TPU v7x, 256 devices: a whole 4x4x8 slice. The times are simulated.
256 devices in a mesh: lon: 128 (over x, y_lo, z, core), lat: 2 (over y_hi).
Axes of the slice: x: 4, y: 4 (y_hi: 2, y_lo: 2; y = y_hi * 2 + y_lo), z: 8, core: 2. Of those that a mesh axis runs over, the one named last changes fastest.
Arguments:
- counts_blocks: int32 [512, 512, 512], P('lon', 'lat'), may hold values from 0 to 49
- exposure_blocks: float32 [512, 512, 512], P('lon', 'lat'), may hold values from 0.1 to 1
- expo_col: int32 [512], P('lon'), may hold values from 0 to 65535, as said below
- expo_count: int32 [128], P('lon'), may hold values from 1 to 4, as said below
Outputs:
- significance: float32 [3, 512, 65536], P(None, 'lat', 'lon')
Inputs may be any that keep to these rules, and one draw needn't show every extreme that they name: `expo_col`: exposure e belongs to lon device i = e // 4; its first sky column is ((i + k) * 512 + o) modulo 65536 with k from -2 to 1 and o from 0 to 511, and its 512 columns run on round the band. Exposures e of lon device i with e modulo 4 below expo_count[i] are observed; the others take no part.
All inputs are finite; a program needn't handle non-finite values.
Results may differ from a plain program's by a relative error of at most 0.00065.
Values sent between devices are 32-bit elements; how exact they have to be, the bound alone decides.
No kernel may reach another device: no remote copies, remote signals or barrier semaphores. Data moves between devices by JAX's collectives and lax.ppermute only.
A program may use at most 128 MiB of HBM per device.

v0:
```python
import jax
import jax.numpy as jnp
from jax import lax
from jax.sharding import PartitionSpec as P

TW = 512
RAD = 32
SCALES = 3
REACH = 2


def padded(block, sides, width, periodic):
    for axis, dim in sides:
        count = lax.axis_size(axis)
        forward = [(i, i + 1) for i in range(count - 1)]
        if periodic:
            forward.append((count - 1, 0))
        backward = [(target, source) for source, target in forward]
        low = lax.ppermute(
            lax.slice_in_dim(block, block.shape[dim] - width, None, axis=dim), axis, forward
        )
        high = lax.ppermute(lax.slice_in_dim(block, 0, width, axis=dim), axis, backward)
        block = jnp.concatenate([low, block, high], axis=dim)
    return block


def from_behind(value, axis, steps):
    count = lax.axis_size(axis)
    pairs = [(source, (source + steps) % count) for source in range(count)]
    return lax.ppermute(value, axis, pairs)


def kernel_pair(offset, sigma):
    inside = (jnp.abs(offset) <= RAD).astype(jnp.float32)
    bell = jnp.exp(-offset * offset / (2.0 * sigma * sigma)) * inside
    hat = (1.0 - offset * offset / (sigma * sigma)) * bell
    return (hat, bell)


def widen(fields):
    taller = padded(fields, (("lat", 1),), RAD, False)
    return padded(taller, (("lon", 2),), RAD, True)


def row_sums(count_rows, expo_rows):
    return lax.psum((count_rows, expo_rows), "lon")


def per_device(counts_blocks, exposure_blocks, expo_col, expo_count):
    slots, rows, block = counts_blocks.shape
    tile = TW
    reach = REACH
    cycle = lax.axis_size("lon")
    mine = lax.axis_index("lon")
    zero = jnp.zeros((), jnp.int32)
    canvases = jnp.zeros((2 * reach, 2, rows, 2 * tile), jnp.float32)
    for slot in range(slots):
        column = expo_col[slot]
        first = column // tile
        within = column % tile
        rel = (first - mine + cycle // 2) % cycle - cycle // 2
        alive = (slot < expo_count[0]).astype(jnp.float32)
        stacked = (
            jnp.stack([counts_blocks[slot].astype(jnp.float32), exposure_blocks[slot]]) * alive
        )
        canvas = lax.dynamic_update_slice(
            jnp.zeros((2, rows, 2 * tile), jnp.float32), stacked, (zero, zero, within)
        )
        place = rel + reach
        current = lax.dynamic_index_in_dim(canvases, place, 0, keepdims=False)
        canvases = lax.dynamic_update_index_in_dim(canvases, current + canvas, place, 0)
    pieces = []
    for offset in range(-reach, reach + 1):
        piece = jnp.zeros((2, rows, tile), jnp.float32)
        if offset <= reach - 1:
            piece = canvases[offset + reach, :, :, :tile]
        if offset >= 1 - reach:
            piece = piece + canvases[offset - 1 + reach, :, :, tile:]
        pieces.append(piece)
    total = pieces[reach]
    for offset in range(-reach, reach + 1):
        if offset != 0:
            total = total + from_behind(pieces[offset + reach], "lon", offset)
    count_rows, expo_rows = row_sums(jnp.sum(total[0], axis=1), jnp.sum(total[1], axis=1))
    rate = count_rows / expo_rows
    back = rate[:, None] * total[1]
    extended = widen(jnp.stack([total[0] - back, back]))
    excess_ext = extended[0]
    back_ext = extended[1]
    col_off = (jnp.arange(tile + 2 * RAD)[:, None] - jnp.arange(tile)[None, :] - RAD).astype(
        jnp.float32
    )
    row_off = (jnp.arange(rows + 2 * RAD)[None, :] - jnp.arange(rows)[:, None] - RAD).astype(
        jnp.float32
    )
    highest = lax.Precision.HIGHEST
    results = []
    for scale in range(SCALES):
        sigma = RAD / 2.0 ** (4 - scale)
        hat_x, bell_x = kernel_pair(col_off, sigma)
        hat_y, bell_y = kernel_pair(row_off, sigma)
        excess_cols = jnp.dot(
            excess_ext, jnp.concatenate([hat_x, bell_x], axis=1), precision=highest
        )
        back_cols = jnp.dot(
            back_ext,
            jnp.concatenate([hat_x * hat_x, hat_x * bell_x, bell_x * bell_x], axis=1),
            precision=highest,
        )
        wavelet = jnp.dot(
            jnp.concatenate([bell_y, hat_y], axis=1),
            jnp.concatenate([excess_cols[:, :tile], excess_cols[:, tile:]], axis=0),
            precision=highest,
        )
        variance = jnp.dot(
            jnp.concatenate([bell_y * bell_y, 2.0 * hat_y * bell_y, hat_y * hat_y], axis=1),
            jnp.concatenate(
                [back_cols[:, :tile], back_cols[:, tile : 2 * tile], back_cols[:, 2 * tile :]],
                axis=0,
            ),
            precision=highest,
        )
        results.append(wavelet / jnp.sqrt(jnp.maximum(variance, 1.0)))
    return jnp.stack(results)


def solution(mesh):
    placed = (P("lon", "lat", None), P("lon", "lat", None), P("lon"), P("lon"))
    return jax.shard_map(
        per_device, mesh=mesh, in_specs=placed, out_specs=P(None, "lat", "lon"), check_vma=False
    )
```

profile of v0, /device:TPU:0, one launch (start us, length us, event | category | flops | bytes accessed | tf_op | source)
XLA Modules:
  0.0 450.2 jit_solution(5886807643575229498)
XLA Ops:
  0.0 1.4 fusion.163
  11.3 2.9 convert_bitcast_fusion
  14.2 1.2 slice_bitcast_fusion.10
  16.4 3.6 dynamic_update_slice.29
  20.1 1.1 broadcast_in_dim.15
  21.5 3.3 copy-done
  25.1 5.9 %dynamic_update_slice.32 = f32[4,2,256,1024]{3,2,1,0:T(8,128)} dynamic-update-slice(f32[4,2,256,1024]{3,2,1,0:T(8,128)} %copy-done, f32[1,2,256,512]{3,2,1,0:T(8,128)S(1)} %fusion.103, s32[]{:T(128)S(6)} %select_n.97, s32[]{:T(128)} %constant.265.clone.1, s32[]{:T(128)} %constant.265.clone.1, s32[]{:T(128)S(6)} %select_n.101) | dynamic-update-slice | bytes 2097156 | tf_op jit(solution)/shard_map/jit(dynamic_update_index_in_dim)/dynamic_update_slice | solution.py:71
  31.0 1.7 fusion.104
  32.7 6.4 %dynamic_update_slice.34 = f32[4,2,256,1024]{3,2,1,0:T(8,128)} dynamic-update-slice(f32[4,2,256,1024]{3,2,1,0:T(8,128)} %dynamic_update_slice.32, f32[1,2,256,512]{3,2,1,0:T(8,128)S(1)} %fusion.104, s32[]{:T(128)S(6)} %select_n.104, s32[]{:T(128)} %constant.265.clone.1, s32[]{:T(128)} %constant.265.clone.1, s32[]{:T(128)S(6)} %select_n.108) | dynamic-update-slice | bytes 2097156 | tf_op jit(solution)/shard_map/jit(dynamic_update_index_in_dim)/dynamic_update_slice | solution.py:71
  39.1 1.7 fusion.105
  40.7 6.4 %dynamic_update_slice.36 = f32[4,2,256,1024]{3,2,1,0:T(8,128)} dynamic-update-slice(f32[4,2,256,1024]{3,2,1,0:T(8,128)} %dynamic_update_slice.34, f32[1,2,256,512]{3,2,1,0:T(8,128)S(1)} %fusion.105, s32[]{:T(128)S(6)} %select_n.111, s32[]{:T(128)} %constant.265.clone.1, s32[]{:T(128)} %constant.265.clone.1, s32[]{:T(128)S(6)} %select_n.115) | dynamic-update-slice | bytes 2097156 | tf_op jit(solution)/shard_map/jit(dynamic_update_index_in_dim)/dynamic_update_slice | solution.py:71
  47.2 3.5 slice_bitcast_fusion.1
  50.7 7.7 %collective-permute-start = (f32[2,256,512]{2,1,0:T(8,128)S(1)}, f32[2,256,512]{2,1,0:T(8,128)S(1)}, u32[]{:S(2)}, u32[]{:S(2)}) collective-permute-start(f32[2,256,512]{2,1,0:T(8,128)S(1)} %get-tuple-element.11), channel_id=1, source_target_pairs={{0,252},{2,254},{4,0},{6,2},{8,4},{10,6},{12,8},{14,10},{16,12},{1... | collective-permute-start | bytes 3145736 | tf_op jit(solution)/shard_map/ppermute | solution.py:30
  58.4 1.1 collective-permute-start.1
  59.5 1.8 collective-permute-start.3
  61.3 1.2 subtract_multiply_fusion.5
  62.4 1.6 fusion.136
  64.1 1.1 multiply_multiply_fusion.2
  65.2 1.0 fusion.142
  66.1 1.1 subtract_multiply_fusion.4
  67.2 0.6 fusion.137
  67.9 1.2 multiply_multiply_fusion.1
  69.1 0.6 fusion.138
  69.7 1.1 subtract_multiply_fusion.3
  70.8 1.0 fusion.143
  71.8 2.0 exponential_select_fusion.2
  73.8 2.1 fusion.130
  75.9 2.0 exponential_select_fusion.1
  77.9 2.1 fusion.132
  80.0 2.2 fusion.134
  82.2 2.0 exponential_select_fusion
  84.2 8.9 %collective-permute-done.1 = f32[2,256,512]{2,1,0:T(8,128)S(1)} collective-permute-done((f32[2,256,512]{2,1,0:T(8,128)S(1)}, f32[2,256,512]{2,1,0:T(8,128)S(1)}, u32[]{:S(2)}, u32[]{:S(2)}) %collective-permute-start.1) | collective-permute-done | bytes 1048608 | tf_op jit(solution)/shard_map/ppermute | solution.py:30
  93.2 2.3 fusion.102
  95.7 282.7 %all-reduce = (f32[256]{0:T(256)S(1)}, f32[256]{0:T(256)S(1)}) all-reduce(f32[256]{0:T(256)S(1)} %get-tuple-element.6, f32[256]{0:T(256)S(1)} %get-tuple-element.5), channel_id=1, replica_groups=mesh['lon'=128,'lat'=2] {'lon'}, use_global_device_ids=true, to_apply=%region_1.2 | all-reduce | flops 512 | bytes 4096 | tf_op jit(solution)/shard_map/psum | solution.py:46
  378.5 4.8 %collective-permute-start.4 = (f32[2,32,512]{2,1,0:T(8,128)S(1)}, f32[2,32,512]{2,1,0:T(8,128)S(1)}, u32[]{:S(2)}, u32[]{:S(2)}) collective-permute-start(f32[2,32,512]{2,1,0:T(8,128)S(1)} %get-tuple-element.40), channel_id=1, source_target_pairs={{0,1},{2,3},{4,5},{6,7},{8,9},{10,11},{12,13},{14,15},{16,17},{18,... | collective-permute-start | bytes 393224 | tf_op jit(solution)/shard_map/ppermute | solution.py:19
  383.3 1.3 collective-permute-start.5
  384.9 0.9 collective-permute-done.4
  385.8 5.9 %collective-permute-done.5 = f32[2,32,512]{2,1,0:T(8,128)S(1)} collective-permute-done((f32[2,32,512]{2,1,0:T(8,128)S(1)}, f32[2,32,512]{2,1,0:T(8,128)S(1)}, u32[]{:S(2)}, u32[]{:S(2)}) %collective-permute-start.5) | collective-permute-done | bytes 131104 | tf_op jit(solution)/shard_map/ppermute | solution.py:22
  392.0 6.1 %collective-permute-start.7 = (f32[2,320,32]{2,1,0:T(8,128)S(1)}, f32[2,320,32]{2,1,0:T(8,128)S(1)}, u32[]{:S(2)}, u32[]{:S(2)}) collective-permute-start(f32[2,320,32]{2,1,0:T(8,128)S(1)} %get-tuple-element.39), channel_id=1, source_target_pairs={{2,0},{4,2},{6,4},{8,6},{10,8},{12,10},{14,12},{16,14},{18,16},{20... | collective-permute-start | bytes 245768 | tf_op jit(solution)/shard_map/ppermute | solution.py:22
  398.3 4.3 collective-permute-done.6
  402.7 0.6 pad_maximum_fusion
  403.3 3.4 fusion.18
  406.8 1.1 copy-done.3
  408.3 4.9 %fusion = f32[320,1536]{1,0:T(8,128)S(1)} fusion(f32[576,512]{1,0:T(8,128)S(1)} %copy-done.10, f32[576,512]{1,0:T(8,128)S(1)} %copy-done.11, f32[576,512]{1,0:T(8,128)S(1)} %copy-done.3, f32[2,320,576]{2,1,0:T(8,128)S(1)} %pad_maximum_fusion), kind=kOutput, calls=%fused_computation | convolution fusion | flops 3399155712 | bytes 6324224 | tf_op jit(solution)/shard_map/dot_general | solution.py:105
  413.4 1.1 copy-done.8
  414.5 0.4 copy-done.9
  414.9 3.4 fusion.22
  418.4 1.1 copy-done.6
  419.5 0.4 copy-done.7
  419.9 5.4 %fusion.6 = f32[320,1536]{1,0:T(8,128)S(1)} fusion(f32[576,512]{1,0:T(8,128)S(1)} %copy-done.6, f32[576,512]{1,0:T(8,128)S(1)} %copy-done.7, f32[576,512]{1,0:T(8,128)S(1)} %fusion.137, f32[2,320,576]{2,1,0:T(8,128)S(1)} %pad_maximum_fusion), kind=kOutput, calls=%fused_computation.6 | convolution fusion | flops 3399155712 | bytes 6324224 | tf_op jit(solution)/shard_map/dot_general | solution.py:105
  425.4 1.1 copy-done.4
  426.5 0.4 copy-done.5
  426.9 4.9 %fusion.12 = f32[320,1536]{1,0:T(8,128)S(1)} fusion(f32[576,512]{1,0:T(8,128)S(1)} %copy-done.4, f32[576,512]{1,0:T(8,128)S(1)} %copy-done.5, f32[576,512]{1,0:T(8,128)S(1)} %fusion.138, f32[2,320,576]{2,1,0:T(8,128)S(1)} %pad_maximum_fusion), kind=kOutput, calls=%fused_computation.12 | convolution fusion | flops 3399155712 | bytes 6324224 | tf_op jit(solution)/shard_map/dot_general | solution.py:105
  432.0 1.1 copy-done.1
  433.1 0.4 copy-done.2
  433.5 3.4 fusion.26
  437.0 0.9 copy-done.21
  438.0 1.5 fusion.48
  439.5 1.7 fusion.52
  441.2 1.5 fusion.56
  442.7 2.0 fusion.93
  444.7 2.0 fusion.81
  446.7 2.0 fusion.69
  448.7 1.3 pad_maximum_fusion.1
  (78 shorter events, 3.4 us)
Async XLA Ops:
  11.3 2.9 copy-start.14
  21.2 3.6 copy-start.19
  21.2 3.6 copy-start.20
  21.4 3.3 copy-start
  25.1 5.9 %copy-start.17 = (f32[1,1,256,512]{3,2,1,0:T(8,128)S(1)}, f32[1,1,256,512]{3,2,1,0:T(8,128)}, u32[]{:S(2)}) copy-start(f32[1,1,256,512]{3,2,1,0:T(8,128)} %get-tuple-element.18) | copy-start | bytes 1572868
  25.1 5.9 %copy-start.18 = (f32[1,1,256,512]{3,2,1,0:T(8,128)S(1)}, f32[1,1,256,512]{3,2,1,0:T(8,128)}, u32[]{:S(2)}) copy-start(f32[1,1,256,512]{3,2,1,0:T(8,128)} %get-tuple-element.22) | copy-start | bytes 1572868
  32.7 6.4 %copy-start.15 = (f32[1,1,256,512]{3,2,1,0:T(8,128)S(1)}, f32[1,1,256,512]{3,2,1,0:T(8,128)}, u32[]{:S(2)}) copy-start(f32[1,1,256,512]{3,2,1,0:T(8,128)} %get-tuple-element.15) | copy-start | bytes 1572868
  32.7 6.4 %copy-start.16 = (f32[1,1,256,512]{3,2,1,0:T(8,128)S(1)}, f32[1,1,256,512]{3,2,1,0:T(8,128)}, u32[]{:S(2)}) copy-start(f32[1,1,256,512]{3,2,1,0:T(8,128)} %get-tuple-element.19) | copy-start | bytes 1572868
  50.7 33.5 %collective-permute-start = (f32[2,256,512]{2,1,0:T(8,128)S(1)}, f32[2,256,512]{2,1,0:T(8,128)S(1)}, u32[]{:S(2)}, u32[]{:S(2)}) collective-permute-start(f32[2,256,512]{2,1,0:T(8,128)S(1)} %get-tuple-element.11), channel_id=1, source_target_pairs={{0,252},{2,254},{4,0},{6,2},{8,4},{10,6},{12,8},{14,10},{16,12},{1... | collective-permute-start | bytes 3145736 | tf_op jit(solution)/shard_map/ppermute | solution.py:30
  58.4 34.8 %collective-permute-start.1 = (f32[2,256,512]{2,1,0:T(8,128)S(1)}, f32[2,256,512]{2,1,0:T(8,128)S(1)}, u32[]{:S(2)}, u32[]{:S(2)}) collective-permute-start(f32[2,256,512]{2,1,0:T(8,128)S(1)} %get-tuple-element.12), channel_id=1, source_target_pairs={{0,254},{2,0},{4,2},{6,4},{8,6},{10,8},{12,10},{14,12},{16,14},{18... | collective-permute-start | bytes 3145736 | tf_op jit(solution)/shard_map/ppermute | solution.py:30
  59.5 33.7 %collective-permute-start.2 = (f32[2,256,512]{2,1,0:T(8,128)S(1)}, f32[2,256,512]{2,1,0:T(8,128)S(1)}, u32[]{:S(2)}, u32[]{:S(2)}) collective-permute-start(f32[2,256,512]{2,1,0:T(8,128)S(1)} %get-tuple-element.13), channel_id=1, source_target_pairs={{0,2},{2,4},{4,6},{6,8},{8,10},{10,12},{12,14},{14,16},{16,18},{18... | collective-permute-start | bytes 3145736 | tf_op jit(solution)/shard_map/ppermute | solution.py:30
  59.5 33.7 %collective-permute-start.3 = (f32[2,256,512]{2,1,0:T(8,128)S(1)}, f32[2,256,512]{2,1,0:T(8,128)S(1)}, u32[]{:S(2)}, u32[]{:S(2)}) collective-permute-start(f32[2,256,512]{2,1,0:T(8,128)S(1)} %get-tuple-element.14), channel_id=1, source_target_pairs={{0,4},{2,6},{4,8},{6,10},{8,12},{10,14},{12,16},{14,18},{16,20},{1... | collective-permute-start | bytes 3145736 | tf_op jit(solution)/shard_map/ppermute | solution.py:30
  378.5 7.3 %collective-permute-start.4 = (f32[2,32,512]{2,1,0:T(8,128)S(1)}, f32[2,32,512]{2,1,0:T(8,128)S(1)}, u32[]{:S(2)}, u32[]{:S(2)}) collective-permute-start(f32[2,32,512]{2,1,0:T(8,128)S(1)} %get-tuple-element.40), channel_id=1, source_target_pairs={{0,1},{2,3},{4,5},{6,7},{8,9},{10,11},{12,13},{14,15},{16,17},{18,... | collective-permute-start | bytes 393224 | tf_op jit(solution)/shard_map/ppermute | solution.py:19
  383.3 8.4 %collective-permute-start.5 = (f32[2,32,512]{2,1,0:T(8,128)S(1)}, f32[2,32,512]{2,1,0:T(8,128)S(1)}, u32[]{:S(2)}, u32[]{:S(2)}) collective-permute-start(f32[2,32,512]{2,1,0:T(8,128)S(1)} %get-tuple-element.41), channel_id=1, source_target_pairs={{1,0},{3,2},{5,4},{7,6},{9,8},{11,10},{13,12},{15,14},{17,16},{19,... | collective-permute-start | bytes 393224 | tf_op jit(solution)/shard_map/ppermute | solution.py:22
  391.9 10.8 %collective-permute-start.6 = (f32[2,320,32]{2,1,0:T(8,128)S(1)}, f32[2,320,32]{2,1,0:T(8,128)S(1)}, u32[]{:S(2)}, u32[]{:S(2)}) collective-permute-start(f32[2,320,32]{2,1,0:T(8,128)S(1)} %get-tuple-element.38), channel_id=1, source_target_pairs={{0,2},{2,4},{4,6},{6,8},{8,10},{10,12},{12,14},{14,16},{16,18},{18... | collective-permute-start | bytes 245768 | tf_op jit(solution)/shard_map/ppermute | solution.py:19
  392.0 10.7 %collective-permute-start.7 = (f32[2,320,32]{2,1,0:T(8,128)S(1)}, f32[2,320,32]{2,1,0:T(8,128)S(1)}, u32[]{:S(2)}, u32[]{:S(2)}) collective-permute-start(f32[2,320,32]{2,1,0:T(8,128)S(1)} %get-tuple-element.39), channel_id=1, source_target_pairs={{2,0},{4,2},{6,4},{8,6},{10,8},{12,10},{14,12},{16,14},{18,16},{20... | collective-permute-start | bytes 245768 | tf_op jit(solution)/shard_map/ppermute | solution.py:22
  398.3 5.0 %copy-start.12 = (f32[576,512]{1,0:T(8,128)S(1)}, f32[576,512]{1,0:T(8,128)}, u32[]{:S(2)}) copy-start(f32[576,512]{1,0:T(8,128)} %get-tuple-element.46) | copy-start | bytes 3538948
  398.3 5.0 %copy-start.13 = (f32[576,512]{1,0:T(8,128)S(1)}, f32[576,512]{1,0:T(8,128)}, u32[]{:S(2)}) copy-start(f32[576,512]{1,0:T(8,128)} %get-tuple-element.47) | copy-start | bytes 3538948
  403.3 3.5 copy-start.11
  406.7 1.3 copy-start.3
  406.7 1.6 copy-start.10
  413.3 1.3 copy-start.8
  413.3 1.6 copy-start.9
  418.3 1.3 copy-start.6
  418.3 1.6 copy-start.7
  425.3 1.3 copy-start.4
  425.3 1.6 copy-start.5
  431.8 1.3 copy-start.1
  431.8 1.6 copy-start.2
  436.8 1.0 copy-start.21
  436.9 1.1 copy-start.22
  438.0 1.5 copy-start.23
  438.0 1.5 copy-start.24
  439.5 1.7 copy-start.25
  439.5 1.7 copy-start.26
  441.2 1.5 copy-start.29
  441.2 1.5 copy-start.30
  441.2 1.5 copy-start.31
  442.7 2.0 copy-start.27
  442.7 2.0 copy-start.28
  442.7 2.0 copy-start.32
where the time goes:
time: 457 us; the launch traced here: 450 us
  blocking collectives  283 us (62%)
  local copies, waits for them, and re-layouts  39 us (9%)
  other arithmetic  38.2 us (8%)
  matrix products  35.9 us (8%)
  starting transfers between devices  22.9 us (5%)
  waiting for transfers between devices  20.1 us (4%)
  between operations  11.4 us (2%)
    psum x1, blocking collectives, row_sums(): return lax.psum((count_rows, expo_rows), 'lon')  283 us
    dynamic_update_slice x4, local copies, waits for them, and re-layouts, per_device(): lax.dynamic_update_index_in_dim(canvases, current + canvas, place, 0)  18.9 us
    dot_general x3, matrix products, per_device(): jnp.dot(back_ext, jnp.concatenate([hat_x * hat_x, hat_x * bell_x, bell_x...  15.2 us
    unnamed x66, local copies, waits for them, and re-layouts  11.7 us
    ppermute x4, starting transfers between devices, from_behind(): return lax.ppermute(value, axis, pairs)  10.6 us
    dot_general x3, matrix products, per_device(): jnp.dot(excess_ext, jnp.concatenate([hat_x, bell_x], axis=1), precision=h...  10.1 us
  transfers between devices with their start and end apart: 8, of which 4 were waited for; matrix products, arithmetic and copies ran while one was open for 5% of the time, Pallas kernels for 0%

commit v1 on v0

v1 whole, which is shorter than its diff:
```python
import functools

import jax
import jax.numpy as jnp
import ml_dtypes
import numpy as np
from jax import lax
from jax.experimental import pallas as pl
from jax.experimental.pallas import tpu as pltpu
from jax.sharding import PartitionSpec as P

TW = 512
RAD = 32
SCALES = 3
LON = 128
HALF = 128
FAR_K = 160
NEAR_K = 192
F32 = jnp.float32
BF16 = jnp.bfloat16


def iota(shape, dim):
    return lax.broadcasted_iota(jnp.int32, shape, dim)


def where_am_i():
    lon = lax.axis_index("lon")
    return lon, lax.rem(lon, 2), lax.axis_index("lat")


def pack(x):
    lane = iota((8, 128), 1)
    parts = []
    for j in range(4):
        a = x[32 * j : 32 * j + 8]
        for m in range(1, 4):
            b = pltpu.roll(x[32 * j + 8 * m : 32 * j + 8 * m + 8], 32 * m, 1)
            a = jnp.where(lane < 32 * m, a, b)
        parts.append(a)
    return jnp.concatenate(parts, axis=1)


def unpack(p):
    parts = []
    for j in range(4):
        v = p[:, 128 * j : 128 * j + 128]
        parts.append(v)
        for m in range(1, 4):
            parts.append(pltpu.roll(v, 128 - 32 * m, 1))
    return jnp.concatenate(parts, axis=0)


def slot_place(cols, slot, lon):
    column = cols[slot]
    first = column // TW
    within = column - first * TW
    rel = lax.rem(first - lon + LON + LON // 2, LON) - LON // 2
    return within, rel


def fetch_scalars(cols_hbm, count_hbm, cols, count, sem):
    copies = [
        pltpu.make_async_copy(cols_hbm, cols, sem.at[0]),
        pltpu.make_async_copy(count_hbm, count, sem.at[1]),
    ]
    for copy in copies:
        copy.start()
    return copies


def sums_kernel(count_hbm, c_hbm, e_hbm, sums, acc, count, cbuf, ebuf, ssem, sem):
    scalar = pltpu.make_async_copy(count_hbm, count, ssem)
    scalar.start()
    copies = []
    for slot in range(4):
        copies.append(pltpu.make_async_copy(c_hbm.at[slot], cbuf.at[slot], sem.at[0, slot]))
        copies.append(pltpu.make_async_copy(e_hbm.at[slot], ebuf.at[slot], sem.at[1, slot]))
    for copy in copies:
        copy.start()
    acc[...] = jnp.zeros(acc.shape, F32)
    scalar.wait()
    for slot in range(4):
        copies[2 * slot].wait()
        copies[2 * slot + 1].wait()

        @pl.when(slot < count[0])
        def _(slot=slot):
            def body(g, carry):
                rows = pl.ds(pl.multiple_of(8 * g, 8), 8)
                for f, buf in ((0, cbuf), (1, ebuf)):
                    x = buf[slot, rows, :].astype(F32)
                    x = (x[:, :128] + x[:, 128:256]) + (x[:, 256:384] + x[:, 384:])
                    acc[f, rows, :] += x
                return carry

            lax.fori_loop(0, 2 * HALF // 8, body, 0, unroll=8)

    for f in range(2):
        for j in range(2):
            block = jnp.transpose(acc[f, 128 * j : 128 * j + 128, :])
            sums[f : f + 1, 128 * j : 128 * j + 128] = jnp.sum(block, axis=0, keepdims=True)


def far_kernel(cols_hbm, count_hbm, cbuf, ebuf, near_out, far_out, cols, count, ssem):
    lon, core, lat = where_am_i()
    scalars = fetch_scalars(cols_hbm, count_hbm, cols, count, ssem)
    wanted = jnp.where(core == 1, 1, -2)
    near_out[...] = jnp.zeros(near_out.shape, F32)
    far_out[...] = jnp.zeros(far_out.shape, F32)
    for copy in scalars:
        copy.wait()
    for slot in range(4):
        within, rel = slot_place(cols, slot, lon)

        @pl.when(jnp.logical_and(slot < count[0], rel == wanted))
        def _(slot=slot, within=within):
            lane = iota((8, 128), 1)

            for out, start in ((near_out, HALF * (1 - lat)), (far_out, HALF * lat)):

                def body(g, carry, out=out, start=start):
                    rows = pl.ds(pl.multiple_of(start + 8 * g, 8), 8)
                    here = pl.ds(pl.multiple_of(8 * g, 8), 8)
                    for f, buf in ((0, cbuf), (1, ebuf)):
                        x = rolled(buf, slot, rows, within)
                        for j in range(4):
                            col = lane + 128 * j
                            keep = jnp.where(core == 1, col - within, within - 1 - col) < 0
                            out[f, here, 128 * j : 128 * j + 128] += jnp.where(keep, x[j], 0.0)
                    return carry

                lax.fori_loop(0, HALF // 8, body, 0, unroll=4)


def rolled(buf, slot, rows, within):
    whole = within // 128
    rest = within - 128 * whole
    first = iota((8, 128), 1) < rest
    turned = []
    for j in range(4):
        block = lax.rem(j + 4 - whole, 4)
        x = buf[slot, rows, pl.ds(pl.multiple_of(128 * block, 128), 128)].astype(F32)
        turned.append(pltpu.roll(x, rest, 1))
    return [jnp.where(first, turned[j - 1], turned[j]) for j in range(4)]


def rest_kernel(
    cols_hbm, count_hbm, cbuf, ebuf, q1n, q1f, q0n, q0f, an, af, token, weight, cols, count, ssem
):
    lon, core, lat = where_am_i()
    for copy in fetch_scalars(cols_hbm, count_hbm, cols, count, ssem):
        copy.wait()
    token[...] = jnp.zeros(token.shape, F32)
    sign = 2 * core - 1
    col = iota((8, TW), 1)
    shifts = []
    for slot in range(4):
        within, rel = slot_place(cols, slot, lon)
        alive = slot < count[0]
        shifts.append(within)
        for k, q in enumerate((1, 0, -1, -2)):
            high = jnp.where(jnp.logical_and(alive, rel * sign == q), 1.0, 0.0).astype(F32)
            low = jnp.where(jnp.logical_and(alive, (rel + 1) * sign == q), 1.0, 0.0).astype(F32)
            weight[4 * slot + k] = jnp.where(col >= within, high, low)
    for q1, q0, a, start in ((q1n, q0n, an, HALF * (1 - lat)), (q1f, q0f, af, HALF * lat)):

        def body(g, carry, q1=q1, q0=q0, a=a, start=start):
            rows = pl.ds(pl.multiple_of(start + 8 * g, 8), 8)
            here = pl.ds(pl.multiple_of(8 * g, 8), 8)
            for f, buf in ((0, cbuf), (1, ebuf)):
                xs = [rolled(buf, slot, rows, shifts[slot]) for slot in range(4)]
                for j in range(4):
                    block = slice(128 * j, 128 * j + 128)
                    outs = (q1.at[f], q0.at[f], a.at[0, f], a.at[1, f])
                    for k, out in enumerate(outs):
                        t = xs[0][j] * weight[k, :, block]
                        for slot in range(1, 4):
                            t = t + xs[slot][j] * weight[4 * slot + k, :, block]
                        out[here, block] = t
            return carry

        lax.fori_loop(0, HALF // 8, body, 0, unroll=4)


def merge_kernel(q1, q0, a, b1, partial, message):
    _, core, _ = where_am_i()
    for f in range(2):
        message[f, :HALF, :] = q1[f] + a[1, f]
        mine = q0[f] + a[0, f] + b1[f]
        partial[f] = mine
        edge = jnp.where(core == 1, pltpu.roll(mine[:, 384:], 32, 1), mine[:, :128])
        message[f, HALF:, :] = pack(edge)


def total_kernel(partial, received, sent, total, outer, inner):
    _, core, _ = where_am_i()
    for f in range(2):
        mine = partial[f] + received[f, :HALF, :]
        total[f] = mine
        near = jnp.where(
            core == 1, sent[f, :HALF, :128], pltpu.roll(sent[f, :HALF, 384:], 32, 1)
        )
        outer[f] = unpack(received[f, HALF:, :]) + near
        edge = jnp.where(core == 1, mine[:, :128], pltpu.roll(mine[:, 384:], 32, 1))
        inner[f] = pack(edge)


def seam(total, outer, inner, core):
    lane = iota((HALF, 128), 1)
    left = jnp.where(core == 1, inner, outer)
    right = jnp.where(core == 1, outer, inner)
    a = jnp.where(lane < 96, pltpu.roll(total[:, 384:], 96, 1), pltpu.roll(right, 96, 1))
    b = jnp.where(lane < 32, left, pltpu.roll(total[:, :128], 32, 1))
    return jnp.concatenate([a, b], axis=1)


def seam_kernel(total, outer, inner, wrap, message):
    _, core, lat = where_am_i()
    rows = pl.ds(pl.multiple_of(96 * (1 - lat), 32), 32)
    for f in range(2):
        wrap[f] = seam(total[f], outer[f], unpack(inner[f]), core)
        message[f, :, :TW] = total[f, rows, :]
        message[f, :, TW:] = wrap[f, rows, :]


def bell_hat(offset, sigma):
    inside = jnp.abs(offset) <= RAD
    d = offset.astype(F32)
    bell = jnp.where(inside, jnp.exp(-d * d / (2.0 * sigma * sigma)), 0.0)
    hat = (1.0 - d * d / (sigma * sigma)) * bell
    return bell, hat


def split(x):
    high = x.astype(BF16)
    return high, (x - high.astype(F32)).astype(BF16)


@functools.cache
def tap_scales():
    t = np.arange(-RAD, RAD + 1, dtype=np.float64)
    table = []
    for s in range(SCALES):
        sigma = RAD / 2.0 ** (4 - s)
        g = np.exp(-t * t / (2.0 * sigma * sigma))
        h = (1.0 - t * t / (sigma * sigma)) * g
        row = []
        for k in (h * h, h * g, g * g):
            c = 1.0 + np.arange(4096) / 4096.0
            error = (k * c[:, None]).astype(ml_dtypes.bfloat16).astype(np.float64) / c[:, None] - k
            cost = np.abs(error.sum(1)) / np.abs(k).sum()
            cost = 4.0 * cost + np.sqrt((error**2).sum(1) / (k**2).sum())
            row.append(float(c[np.argmin(cost)]))
        table.append(row)
    return table


def taps_kernel(ctap, cvar, far_tap, near_tap, far_var, near_var, token):
    _, _, lat = where_am_i()
    token[...] = jnp.zeros(token.shape, F32)
    w = iota((256, 128), 0)
    n = iota((256, 128), 1)
    straight = w - n - 64
    wrapped_w = jnp.where(w < 128, 416 + w, w - 160)
    wrapped_n = jnp.where(n < 64, 448 + n, n - 64)
    a = iota((HALF, 128), 0)
    b = iota((HALF, 128), 1)
    table = tap_scales()

    def far_row(p):
        return jnp.where(lat == 0, p, jnp.where(p < HALF, p + HALF, p - 32))

    def near_row(p):
        inner = jnp.where(lat == 0, p + HALF, p)
        adjacent = jnp.where(lat == 0, p - 32, p)
        halo = jnp.where(lat == 0, p + 96, p - 192)
        return jnp.where(p < HALF, inner, jnp.where(p < HALF + 32, adjacent, halo))

    for s in range(SCALES):
        sigma = RAD / 2.0 ** (4 - s)
        chh, chg, cgg = table[s]
        for kind, offset in ((0, straight), (1, wrapped_w - wrapped_n)):
            bell, hat = bell_hat(offset, sigma)
            for k, t in enumerate((hat, bell)):
                high, low = split(t)
                here = slice(256 * s + 128 * k, 256 * s + 128 * k + 128)
                ctap[kind, :256, here] = high
                ctap[kind, 256:512, here] = high
                ctap[kind, 512:, here] = low
            for k, t in enumerate((chh * hat * hat, chg * hat * bell, cgg * bell * bell)):
                here = slice(384 * s + 128 * k, 384 * s + 128 * k + 128)
                t = t.astype(BF16)
                cvar[kind, :256, here] = t
                cvar[kind, 256:, here] = t
        for tap, var, span, place in (
            (far_tap, far_var, FAR_K, far_row),
            (near_tap, near_var, NEAR_K, near_row),
        ):
            for j in range(-(-6 * span // 128)):
                here = slice(128 * j, min(128 * j + 128, 6 * span))
                size = here.stop - here.start
                lane = 128 * j + b
                copy = (lane >= 2 * span).astype(jnp.int32) + (lane >= 4 * span).astype(jnp.int32)
                p = lane - 2 * span * copy
                second = p >= span
                bell, hat = bell_hat(place(jnp.where(second, p - span, p)) - place(a), sigma)
                high, low = split(jnp.where(second, hat, bell))
                t = jnp.where(copy == 1, low.astype(F32), high.astype(F32)).astype(BF16)
                tap[s, :, here] = t[:, :size]
                p = jnp.where(lane >= 3 * span, lane - 3 * span, lane)
                which = (p >= span).astype(jnp.int32) + (p >= 2 * span).astype(jnp.int32)
                bell, hat = bell_hat(place(p - span * which) - place(a), sigma)
                t = jnp.where(which == 1, (2.0 * chg) * hat * bell, chh * hat * hat)
                t = jnp.where(which == 0, cgg * bell * bell, t).astype(BF16)
                var[s, :, here] = t[:, :size]


def mm(a, b):
    return jnp.dot(a, b, preferred_element_type=F32)


def column_filters(size, fields, ctap, cvar, wave, vari, x, xw):
    for j in range(6):
        for f in range(2):
            high, low = split(fields(f, j))
            if j < 4:
                places = [(x, 3 * f + b, j - b) for b in range(3) if j - b in (0, 1)]
            else:
                places = [(xw, f, j - 4)]
            for ref, b, side in places:
                rows = slice(size * b, size * b + size)
                ref[rows, 128 * side : 128 * side + 128] = high
                ref[rows, 256 + 128 * side : 384 + 128 * side] = low
                ref[rows, 512 + 128 * side : 640 + 128 * side] = high
    for f in range(2):
        y = mm(x[3 * size * f : 3 * size * (f + 1), :], ctap[0])
        for s in range(SCALES):
            for k in range(2):
                for b in range(3):
                    wave[s, 2 * f + k, :, 128 * b : 128 * b + 128] = y[
                        size * b : size * b + size, 256 * s + 128 * k : 256 * s + 128 * k + 128
                    ]
    z = mm(x[3 * size :, :512], cvar[0])
    for s in range(SCALES):
        for k in range(3):
            for b in range(3):
                vari[s, k, :, 128 * b : 128 * b + 128] = z[
                    size * b : size * b + size, 384 * s + 128 * k : 384 * s + 128 * k + 128
                ]
    y = mm(xw[...], ctap[1])
    z = mm(xw[size:, :512], cvar[1])
    for s in range(SCALES):
        for k in range(2):
            here = slice(256 * s + 128 * k, 256 * s + 128 * k + 128)
            wave[s, k, :, 384:] = y[:size, here]
            wave[s, 2 + k, :, 384:] = y[size:, here]
        for k in range(3):
            vari[s, k, :, 384:] = z[:, 384 * s + 128 * k : 384 * s + 128 * k + 128]


def near_columns_kernel(total, wrap, ctap, cvar, wave, vari, token, x, xw):
    token[...] = jnp.zeros(token.shape, F32)

    def fields(f, j):
        if j < 4:
            return total[f, :, 128 * j : 128 * j + 128]
        return wrap[f, :, 128 * (j - 4) : 128 * (j - 3)]

    column_filters(HALF, fields, ctap, cvar, wave, vari, x, xw)


def far_columns_kernel(total, outer, inner, lat_rows, ctap, cvar, wave, vari, x, xw):
    _, core, _ = where_am_i()
    wrap = [seam(total[f], outer[f], unpack(inner[f]), core) for f in range(2)]

    def fields(f, j):
        if j < 4:
            mine = total[f, :, 128 * j : 128 * j + 128]
        else:
            mine = wrap[f][:, 128 * (j - 4) : 128 * (j - 3)]
        return jnp.concatenate([mine, lat_rows[f, :, 128 * j : 128 * j + 128]], axis=0)

    column_filters(HALF + RAD, fields, ctap, cvar, wave, vari, x, xw)


def final_kernel(
    near_wave, near_vari, far_wave, far_vari, sums, last,
    far_tap, near_tap, far_var, near_var, out, rate, fw, fv, nw, nv,
):
    _, core, lat = where_am_i()
    whole = sums[...] + last[...]
    own = whole[0:1] / whole[1:2]
    other = whole[2:3] / whole[3:4]
    table = tap_scales()

    def column(row):
        return jnp.transpose(jnp.broadcast_to(row, (128, 128)))

    lo, hi = own[:, :128], own[:, 128:]
    rate[0] = column(jnp.where(lat == 0, lo, hi))
    rate[1] = column(jnp.where(lat == 0, hi, lo))
    halo = column(jnp.where(lat == 0, other[:, :128], other[:, 128:]))
    rate[2, :RAD] = jnp.where(lat == 0, halo[:RAD], halo[96:])
    near_edge = pl.ds(pl.multiple_of(96 * lat, 32), RAD)
    far_edge = pl.ds(pl.multiple_of(96 * (1 - lat), 32), RAD)
    all_rows = slice(0, HALF)
    halo_rows = slice(HALF, HALF + RAD)
    far_parts = ((0, all_rows, 0, all_rows, 0), (1, near_edge, 1, near_edge, HALF))
    near_parts = (
        (1, all_rows, 1, all_rows, 0),
        (0, far_edge, 0, far_edge, HALF),
        (0, halo_rows, 2, slice(0, RAD), HALF + RAD),
    )
    waves = (far_wave, near_wave)
    varis = (far_vari, near_vari)

    for s in range(SCALES):
        factor = [1.0 / (table[s][0] * table[s][2]), 1.0 / table[s][1] ** 2]
        factor.append(factor[0])
        slot = s % 2
        for parts, span, w, v, tap, var, start in (
            (far_parts, FAR_K, fw, fv, far_tap, far_var, HALF * lat),
            (near_parts, NEAR_K, nw, nv, near_tap, near_var, HALF * (1 - lat)),
        ):
            for source, rows, which, rrows, at in parts:
                size = HALF if at == 0 else RAD
                r = rate[which, rrows, :]
                for j in range(4):
                    cols = slice(128 * j, 128 * j + 128)
                    for k in range(2):
                        t = waves[source][s, k, rows, cols] - r * waves[source][s, 2 + k, rows, cols]
                        high, low = split(t)
                        for copy, t in ((0, high), (1, high), (2, low)):
                            first = span * (2 * copy + k) + at
                            w[slot, first : first + size, cols] = t
                    for k in range(3):
                        t = varis[source][s, k, rows, cols] * (r * factor[k])
                        for copy, t in enumerate(split(t)):
                            first = span * (3 * copy + k) + at
                            v[slot, first : first + size, cols] = t
            wavelet = mm(tap[s], w[slot])
            variance = mm(var[s], v[slot])
            signal = wavelet * lax.rsqrt(jnp.maximum(variance, 1.0))
            there = pl.ds(pl.multiple_of(start, HALF), HALF)
            out[s, there, :] = pltpu.roll(signal, 64, 1)


VMEM = pl.BlockSpec(memory_space=pltpu.VMEM)
ANY = pl.BlockSpec(memory_space=pl.ANY)


def call(kernel, outs, ins, scratch=(), after=(), us=0.01, limit=36):
    count = len(ins)

    def body(*refs):
        kernel(*refs[:count], *refs[count + len(after) :])

    def run(*operands):
        return pl.pallas_call(
            body,
            out_shape=[jax.ShapeDtypeStruct(shape, dtype) for shape, dtype in outs],
            in_specs=list(ins) + [ANY] * len(after),
            out_specs=[VMEM] * len(outs),
            scratch_shapes=list(scratch),
            compiler_params=pltpu.CompilerParams(vmem_limit_bytes=limit * 1024 * 1024),
            cost_estimate=pl.CostEstimate(
                flops=0, bytes_accessed=int(us * 3.6e6), transcendentals=0
            ),
        )(*operands, *after)

    return run


TOKEN = (4, 2 * HALF)
TAPS = [
    ((2, 768, 256 * SCALES), BF16),
    ((2, 512, 384 * SCALES), BF16),
    ((SCALES, HALF, 6 * FAR_K), BF16),
    ((SCALES, HALF, 6 * NEAR_K), BF16),
    ((SCALES, HALF, 6 * FAR_K), BF16),
    ((SCALES, HALF, 6 * NEAR_K), BF16),
]
FINAL_SCRATCH = [pltpu.VMEM((3, HALF, 128), F32)] + [
    pltpu.VMEM((2, 6 * span, TW), BF16) for span in (FAR_K, FAR_K, NEAR_K, NEAR_K)
]


def columns_scratch(rows):
    return [pltpu.VMEM((6 * rows, 768), BF16), pltpu.VMEM((2 * rows, 768), BF16)]


def columns_out(rows):
    return [((SCALES, 4, rows, TW), F32), ((SCALES, 3, rows, TW), F32)]


def per_device(counts_blocks, exposure_blocks, expo_col, expo_count):
    piece = (2, HALF, TW)
    blocks = (4, 2 * HALF, TW)

    def on_lon(value, step):
        return lax.ppermute(value, "lon", [(i, step(i) % LON) for i in range(LON)])

    def two_out(i):
        return i + 2 if i % 2 else i - 2

    def one_out(i):
        return i + 1 if i % 2 else i - 1

    def partner(i):
        return i ^ 1

    inputs = (expo_col, expo_count, counts_blocks, exposure_blocks)
    scalars = [pltpu.SMEM((4,), jnp.int32), pltpu.SMEM((1,), jnp.int32)]
    semaphores = [pltpu.SemaphoreType.DMA((2,)), pltpu.SemaphoreType.DMA((2, 4))]
    (sums,) = call(
        sums_kernel,
        [((2, 2 * HALF), F32)],
        [ANY] * 3,
        [pltpu.VMEM((2, 2 * HALF, 128), F32), scalars[1]]
        + [pltpu.VMEM(blocks, jnp.int32), pltpu.VMEM(blocks, F32)]
        + [pltpu.SemaphoreType.DMA(()), semaphores[1]],
        limit=58,
    )(*inputs[1:])
    sums = sums + on_lon(sums, partner)
    rest = call(
        rest_kernel,
        [(piece, F32)] * 4 + [((2,) + piece, F32)] * 2 + [(TOKEN, F32)],
        [ANY, ANY, VMEM, VMEM],
        [pltpu.VMEM((16, 8, TW), F32)] + scalars + semaphores[:1],
        after=[sums],
        us=3.0,
        limit=24,
    )
    q1n, q1f, q0n, q0f, an, af, rest_token = rest(*inputs)
    an = on_lon(an, partner)
    af = on_lon(af, partner)
    other = lax.ppermute(sums, "lat", [(0, 1), (1, 0)])
    sums = jnp.concatenate([sums, other], axis=0) + rest_token
    far_n, far_f = call(
        far_kernel,
        [(piece, F32), (piece, F32)],
        [ANY, ANY, VMEM, VMEM],
        scalars + semaphores[:1],
        after=[sums],
        us=1.5,
        limit=24,
    )(*inputs)
    b1_n = on_lon(far_n, two_out)
    b1_f = on_lon(far_f, two_out)
    steps = [sums]
    sums = sums + on_lon(sums, lambda i: i ^ 16)
    steps.append(sums)
    ctap, cvar, far_tap, near_tap, far_var, near_var, taps_token = call(
        taps_kernel, TAPS + [(TOKEN, F32)], [], after=[steps[1]], us=3.0
    )()
    for flip in (32, 64, 2):
        sums = sums + on_lon(sums, lambda i: i ^ flip)
        if flip == 64:
            sums = sums + taps_token
        steps.append(sums)

    def merge(after, *pieces):
        return call(
            merge_kernel,
            [(piece, F32), ((2, HALF + 8, TW), F32)],
            [VMEM] * 4,
            after=after,
        )(*pieces)

    def totals(after, *pieces):
        return call(
            total_kernel,
            [(piece, F32), ((2, HALF, 128), F32), ((2, 8, TW), F32)],
            [VMEM] * 3,
            after=after,
        )(*pieces)

    partial_n, sent_n = merge([steps[2]], q1n, q0n, an, b1_n)
    b2_n = on_lon(sent_n, one_out)
    partial_f, sent_f = merge([steps[2]], q1f, q0f, af, b1_f)
    b2_f = on_lon(sent_f, one_out)
    total_n, outer_n, inner_n = totals([steps[3]], partial_n, b2_n, sent_n)
    inner_n = on_lon(inner_n, partner)
    wrap_n, message = call(
        seam_kernel, [((2, HALF, 256), F32), ((2, RAD, TW + 256), F32)], [VMEM] * 3
    )(total_n, outer_n, inner_n)
    lat_rows = lax.ppermute(message, "lat", [(0, 1), (1, 0)])
    near_wave, near_vari, near_token = call(
        near_columns_kernel,
        columns_out(HALF) + [(TOKEN, F32)],
        [VMEM] * 4,
        columns_scratch(HALF),
        us=4.0,
    )(total_n, wrap_n, ctap, cvar)
    sums = sums + near_token
    sums = sums + on_lon(sums, lambda i: i ^ 4)
    last = on_lon(sums, lambda i: i ^ 8)
    total_f, outer_f, inner_f = totals([steps[4]], partial_f, b2_f, sent_f)
    inner_f = on_lon(inner_f, partner)
    far_wave, far_vari = call(
        far_columns_kernel,
        columns_out(HALF + RAD),
        [VMEM] * 6,
        columns_scratch(HALF + RAD),
        us=5.0,
    )(total_f, outer_f, inner_f, lat_rows, ctap, cvar)
    (out,) = call(
        final_kernel, [((SCALES, 2 * HALF, TW), F32)], [VMEM] * 10, FINAL_SCRATCH
    )(near_wave, near_vari, far_wave, far_vari, sums, last, far_tap, near_tap, far_var, near_var)
    return out


def solution(mesh):
    placed = (P("lon", "lat", None), P("lon", "lat", None), P("lon"), P("lon"))
    return jax.shard_map(
        per_device, mesh=mesh, in_specs=placed, out_specs=P(None, "lat", "lon"), check_vma=False
    )
```

time: 457 us -> 72.8 us (0.16)
  the two profiles are of different devices: /device:TPU:0 before, /device:TPU:1 now
where the time goes in v1:
time: 72.8 us; the launch traced here: 72.7 us
  starting transfers between devices  25.6 us (35%)
  Pallas kernels  23.7 us (33%)
  waiting for transfers between devices  21.6 us (30%)
  between operations  0.97 us (1%)
    pallas_call x12, Pallas kernels, run(): pl.pallas_call(body, out_shape=[jax.ShapeDtypeStruct(shape, dtype) for sh...  23.7 us
    ppermute x15, starting transfers between devices, on_lon(): return lax.ppermute(value, 'lon', [(i, step(i) % LON) for i in range(LON)])  21.7 us
    ppermute x15, waiting for transfers between devices, on_lon(): return lax.ppermute(value, 'lon', [(i, step(i) % LON) for i in range(LON)])  18.9 us
    ppermute x1, waiting for transfers between devices, per_device(): other = lax.ppermute(sums, 'lat', [(0, 1), (1, 0)])  2.76 us
    ppermute x1, starting transfers between devices, per_device(): lat_rows = lax.ppermute(message, 'lat', [(0, 1), (1, 0)])  2.71 us
  transfers between devices with their start and end apart: 17, of which 10 were waited for; matrix products, arithmetic and copies ran while one was open for 0% of the time, Pallas kernels for 15%

profile of v1, /device:TPU:1, one launch (start us, length us, event | category | flops | bytes accessed | tf_op | source)
XLA Modules:
  0.0 72.7 jit_solution(12840470703405032928)
XLA Ops:
  0.0 0.0 copy-start
  0.0 0.0 copy-start.1
  0.0 0.0 copy-start.2
  0.8 3.4 %shard_map.46 = f32[2,256]{1,0:T(2,128)} custom-call(s32[1]{0:T(128)S(6)} %copy.5.refs_0_.refs_1_, s32[4,256,512]{2,1,0:T(8,128)} %refs_2_.5, f32[4,256,512]{2,1,0:T(8,128)} %refs_3_.3), custom_call_target="tpu_custom_call" | custom-call | bytes 36000 | tf_op jit(solution)/shard_map/pallas_call | solution.py:460
  4.2 3.3 %collective-permute-start = (f32[2,256]{1,0:T(2,128)}, f32[2,256]{1,0:T(2,128)S(1)}, u32[]{:S(2)}, u32[]{:S(2)}) collective-permute-start(f32[2,256]{1,0:T(2,128)} %shard_map.46), channel_id=1, source_target_pairs={{0,2},{2,0},{4,6},{6,4},{8,10},{10,8},{12,14},{14,12},{16,18},{18,... | collective-permute-start | bytes 6152 | tf_op jit(solution)/shard_map/ppermute | solution.py:502
  7.5 1.0 %collective-permute-done = f32[2,256]{1,0:T(2,128)S(1)} collective-permute-done((f32[2,256]{1,0:T(2,128)}, f32[2,256]{1,0:T(2,128)S(1)}, u32[]{:S(2)}, u32[]{:S(2)}) %collective-permute-start) | collective-permute-done | bytes 2080 | tf_op jit(solution)/shard_map/ppermute | solution.py:502
  8.5 0.7 add.27.refs_4_
  9.2 0.0 copy-done
  9.2 0.0 copy-done.1
  9.2 0.0 copy-done.2
  9.2 2.9 %shard_map.47 = (f32[2,128,512]{2,1,0:T(8,128)S(1)}, f32[2,128,512]{2,1,0:T(8,128)S(1)}, f32[2,128,512]{2,1,0:T(8,128)S(1)}, f32[2,128,512]{2,1,0:T(8,128)S(1)},...) custom-call(s32[4]{0:T(128)S(1)} %copy-done.2, s32[1]{0:T(128)S(6)} %copy.5.refs_0_.refs_1_, ...), custom_call_target="tpu_custom_call" | custom-call | bytes 10800000 | tf_op jit(solution)/shard_map/pallas_call | solution.py:460
  12.2 0.4 collective-permute-start.1
  12.6 0.2 collective-permute-start.9
  12.8 1.2 %collective-permute-start.2 = (f32[2,256]{1,0:T(2,128)S(1)}, f32[2,256]{1,0:T(2,128)S(1)}, u32[]{:S(2)}, u32[]{:S(2)}) collective-permute-start(f32[2,256]{1,0:T(2,128)S(1)} %add.27.refs_4_), channel_id=1, source_target_pairs={{0,1},{1,0},{2,3},{3,2},{4,5},{5,4},{6,7},{7,6},{8,9},{9,8},{10,11... | collective-permute-start | bytes 6152 | tf_op jit(solution)/shard_map/ppermute | solution.py:538
  13.9 2.8 %collective-permute-done.2 = f32[2,256]{1,0:T(2,128)S(1)} collective-permute-done((f32[2,256]{1,0:T(2,128)S(1)}, f32[2,256]{1,0:T(2,128)S(1)}, u32[]{:S(2)}, u32[]{:S(2)}) %collective-permute-start.2) | collective-permute-done | bytes 2080 | tf_op jit(solution)/shard_map/ppermute | solution.py:538
  16.7 1.6 %shard_map.48 = (f32[2,128,512]{2,1,0:T(8,128)S(1)}, f32[2,128,512]{2,1,0:T(8,128)S(1)}) custom-call(s32[4]{0:T(128)S(1)} %copy-done.2, s32[1]{0:T(128)S(6)} %copy.5.refs_0_.refs_1_, s32[4,256,512]{2,1,0:T(8,128)S(1)} %copy-done, f32[4,256,512]{2,1,0:T(8,128)S(1)} %copy-done.1, f32[4,256]{1,0:T(4,128)S(1)} %maximum_add_fusion.refs_4_), custom_call_target="tpu_custom_call" | custom-call | bytes 5400000 | tf_op jit(solution)/shard_map/pallas_call | solution.py:460
  18.3 0.1 collective-permute-start.3
  18.4 0.6 collective-permute-start.10
  19.0 1.3 %collective-permute-start.4 = (f32[4,256]{1,0:T(4,128)S(1)}, f32[4,256]{1,0:T(4,128)S(1)}, u32[]{:S(2)}, u32[]{:S(2)}) collective-permute-start(f32[4,256]{1,0:T(4,128)S(1)} %maximum_add_fusion.refs_4_), channel_id=1, source_target_pairs={{0,32},{2,34},{4,36},{6,38},{8,40},{10,42},{12,44},{14,46},{16,48}... | collective-permute-start | bytes 12296 | tf_op jit(solution)/shard_map/ppermute | solution.py:502
  20.3 1.1 %collective-permute-done.4 = f32[4,256]{1,0:T(4,128)S(1)} collective-permute-done((f32[4,256]{1,0:T(4,128)S(1)}, f32[4,256]{1,0:T(4,128)S(1)}, u32[]{:S(2)}, u32[]{:S(2)}) %collective-permute-start.4) | collective-permute-done | bytes 4128 | tf_op jit(solution)/shard_map/ppermute | solution.py:502
  21.5 4.5 %collective-permute-start.5 = (f32[4,256]{1,0:T(4,128)S(1)}, f32[4,256]{1,0:T(4,128)S(1)}, u32[]{:S(2)}, u32[]{:S(2)}) collective-permute-start(f32[4,256]{1,0:T(4,128)S(1)} %add.29.refs_0_), channel_id=1, source_target_pairs={{0,64},{2,66},{4,68},{6,70},{8,72},{10,74},{12,76},{14,78},{16,80}... | collective-permute-start | bytes 12296 | tf_op jit(solution)/shard_map/ppermute | solution.py:502
  26.0 1.3 %collective-permute-done.5 = f32[4,256]{1,0:T(4,128)S(1)} collective-permute-done((f32[4,256]{1,0:T(4,128)S(1)}, f32[4,256]{1,0:T(4,128)S(1)}, u32[]{:S(2)}, u32[]{:S(2)}) %collective-permute-start.5) | collective-permute-done | bytes 4128 | tf_op jit(solution)/shard_map/ppermute | solution.py:502
  27.3 4.7 %collective-permute-done.3.refs_3_ = f32[2,128,512]{2,1,0:T(8,128)S(1)} collective-permute-done((f32[2,128,512]{2,1,0:T(8,128)S(1)}, f32[2,128,512]{2,1,0:T(8,128)S(1)}, u32[]{:S(2)}, u32[]{:S(2)}) %collective-permute-start.3) | collective-permute-done | bytes 524320 | tf_op jit(solution)/shard_map/ppermute | solution.py:502
  32.1 0.0 collective-permute-done.1.refs_2_
  32.1 0.2 shard_map.49
  32.3 3.2 %collective-permute-start.6 = (f32[2,136,512]{2,1,0:T(8,128)S(1)}, f32[2,136,512]{2,1,0:T(8,128)S(1)}, u32[]{:S(2)}, u32[]{:S(2)}) collective-permute-start(f32[2,136,512]{2,1,0:T(8,128)S(1)} %get-tuple-element.44.refs_2_), channel_id=1, source_target_pairs={{0,254},{2,4},{4,2},{6,8},{8,6},{10,12},{12,10},{14,16},{16,14},{1... | collective-permute-start | bytes 1671176 | tf_op jit(solution)/shard_map/ppermute | solution.py:502
  35.5 2.2 %collective-permute-done.10.refs_3_ = f32[2,128,512]{2,1,0:T(8,128)S(1)} collective-permute-done((f32[2,128,512]{2,1,0:T(8,128)S(1)}, f32[2,128,512]{2,1,0:T(8,128)S(1)}, u32[]{:S(2)}, u32[]{:S(2)}) %collective-permute-start.10) | collective-permute-done | bytes 524320 | tf_op jit(solution)/shard_map/ppermute | solution.py:502
  37.7 0.0 collective-permute-done.9.refs_2_
  37.7 0.2 shard_map.54
  37.9 0.1 collective-permute-start.11
  38.0 0.8 %collective-permute-start.7 = (f32[4,256]{1,0:T(4,128)S(1)}, f32[4,256]{1,0:T(4,128)S(1)}, u32[]{:S(2)}, u32[]{:S(2)}) collective-permute-start(f32[4,256]{1,0:T(4,128)S(1)} %add.30.refs_4_), channel_id=1, source_target_pairs={{0,128},{2,130},{4,132},{6,134},{8,136},{10,138},{12,140},{14,142}... | collective-permute-start | bytes 12296 | tf_op jit(solution)/shard_map/ppermute | solution.py:502
  38.8 3.5 %shard_map.50 = (bf16[2,768,768]{2,1,0:T(8,128)(2,1)S(1)}, bf16[2,512,1152]{2,1,0:T(8,128)(2,1)S(1)}, bf16[3,128,960]{2,1,0:T(8,128)(2,1)S(1)}, bf16[3,128,1152]...) custom-call(f32[4,256]{1,0:T(4,128)S(1)} %add.29.refs_0_), custom_call_target="tpu_custom_call" | custom-call | bytes 10800000 | tf_op jit(solution)/shard_map/pallas_call | solution.py:460
  42.3 0.0 collective-permute-done.7
  42.3 0.6 collective-permute-done.6.refs_1_
  43.0 0.2 shard_map.51
  43.2 6.5 %collective-permute-start.8 = (f32[2,8,512]{2,1,0:T(8,128)S(1)}, f32[2,8,512]{2,1,0:T(8,128)S(1)}, u32[]{:S(2)}, u32[]{:S(2)}) collective-permute-start(f32[2,8,512]{2,1,0:T(8,128)S(1)} %get-tuple-element.48), channel_id=1, source_target_pairs={{0,2},{2,0},{4,6},{6,4},{8,10},{10,8},{12,14},{14,12},{16,18},{18,... | collective-permute-start | bytes 98312 | tf_op jit(solution)/shard_map/ppermute | solution.py:502
  49.7 0.0 collective-permute-start.12
  49.7 0.9 %collective-permute-done.8.refs_2_ = f32[2,8,512]{2,1,0:T(8,128)S(1)} collective-permute-done((f32[2,8,512]{2,1,0:T(8,128)S(1)}, f32[2,8,512]{2,1,0:T(8,128)S(1)}, u32[]{:S(2)}, u32[]{:S(2)}) %collective-permute-start.8) | collective-permute-done | bytes 32800 | tf_op jit(solution)/shard_map/ppermute | solution.py:502
  50.6 0.2 shard_map.52
  50.8 2.7 %collective-permute-start.14 = (f32[2,32,768]{2,1,0:T(8,128)S(1)}, f32[2,32,768]{2,1,0:T(8,128)S(1)}, u32[]{:S(2)}, u32[]{:S(2)}) collective-permute-start(f32[2,32,768]{2,1,0:T(8,128)S(1)} %get-tuple-element.63), channel_id=1, source_target_pairs={{0,1},{1,0},{2,3},{3,2},{4,5},{5,4},{6,7},{7,6},{8,9},{9,8},{10,11... | collective-permute-start | bytes 589832 | tf_op jit(solution)/shard_map/ppermute | solution.py:588
  53.5 2.3 %shard_map.53 = (f32[3,4,128,512]{3,2,1,0:T(8,128)S(1)}, f32[3,3,128,512]{3,2,1,0:T(8,128)S(1)}, f32[4,256]{1,0:T(4,128)S(1)}) custom-call(f32[2,128,512]{2,1,0:T(8,128)S(1)} %get-tuple-element.46.refs_0_, f32[2,128,256]{2,1,0:T(8,128)S(1)} %get-tuple-element.49.refs_1_, bf16[2,768,768]{2,1,0:T(8,128)(2,1)S(1)} %get-tuple-element.50.refs_2_.refs_4_, ...), custom_call_target="tpu_custom_call" | custom-call | bytes 14400000 | tf_op jit(solution)/shard_map/pallas_call | solution.py:460
  55.7 0.0 collective-permute-done.12
  55.8 0.0 collective-permute-done.11.refs_1_
  55.8 0.2 shard_map.55
  56.0 0.7 collective-permute-start.13
  56.7 0.0 collective-permute-start.15
  56.7 3.4 %collective-permute-done.15 = f32[4,256]{1,0:T(4,128)S(1)} collective-permute-done((f32[4,256]{1,0:T(4,128)S(1)}, f32[4,256]{1,0:T(4,128)S(1)}, u32[]{:S(2)}, u32[]{:S(2)}) %collective-permute-start.15) | collective-permute-done | bytes 4128 | tf_op jit(solution)/shard_map/ppermute | solution.py:502
  60.1 0.0 collective-permute-start.16
  60.1 0.0 collective-permute-done.13.refs_2_
  60.1 0.0 collective-permute-done.14.refs_3_
  60.1 2.8 %shard_map.56 = (f32[3,4,160,512]{3,2,1,0:T(8,128)S(1)}, f32[3,3,160,512]{3,2,1,0:T(8,128)S(1)}) custom-call(f32[2,128,512]{2,1,0:T(8,128)S(1)} %get-tuple-element.60.refs_0_, f32[2,128,128]{2,1,0:T(8,128)S(1)} %get-tuple-element.61.refs_1_, f32[2,8,512]{2,1,0:T(8,128)S(1)} %collective-permute-done.13.refs_2_, ...), custom_call_target="tpu_custom_call" | custom-call | bytes 18000000 | tf_op jit(solution)/shard_map/pallas_call | solution.py:460
  62.9 3.6 %collective-permute-done.16.refs_5_ = f32[4,256]{1,0:T(4,128)S(1)} collective-permute-done((f32[4,256]{1,0:T(4,128)S(1)}, f32[4,256]{1,0:T(4,128)S(1)}, u32[]{:S(2)}, u32[]{:S(2)}) %collective-permute-start.16) | collective-permute-done | bytes 4128 | tf_op jit(solution)/shard_map/ppermute | solution.py:502
  66.5 6.2 %shard_map.57 = f32[3,256,512]{2,1,0:T(8,128)} custom-call(f32[3,4,128,512]{3,2,1,0:T(8,128)S(1)} %get-tuple-element.52.refs_0_, f32[3,3,128,512]{3,2,1,0:T(8,128)S(1)} %get-tuple-element.53.refs_1_, f32[3,4,160,512]{3,2,1,0:T(8,128)S(1)} %get-tuple-element.64.refs_2_, f32[3,3,160,512]{3,2,1,0:T(8,128)S(1)} %get-tuple-element.65.refs_3_, ...), custom_call_target="tpu_custom_call" | custom-call | bytes 36000 | tf_op jit(solution)/shard_map/pallas_call | solution.py:460
  (6 shorter events, 0.0 us)
Async XLA Ops:
  0.0 9.2 %copy-start = (s32[4,256,512]{2,1,0:T(8,128)S(1)}, s32[4,256,512]{2,1,0:T(8,128)}, u32[]{:S(2)}) copy-start(s32[4,256,512]{2,1,0:T(8,128)} %refs_2_.5) | copy-start | bytes 6291460
  0.0 9.2 %copy-start.1 = (f32[4,256,512]{2,1,0:T(8,128)S(1)}, f32[4,256,512]{2,1,0:T(8,128)}, u32[]{:S(2)}) copy-start(f32[4,256,512]{2,1,0:T(8,128)} %refs_3_.3) | copy-start | bytes 6291460
  0.0 9.2 %copy-start.2 = (s32[4]{0:T(128)S(1)}, s32[4]{0:T(128)}, u32[]{:S(2)}) copy-start(s32[4]{0:T(128)} %refs_0_.4) | copy-start | bytes 52
  4.2 4.4 %collective-permute-start = (f32[2,256]{1,0:T(2,128)}, f32[2,256]{1,0:T(2,128)S(1)}, u32[]{:S(2)}, u32[]{:S(2)}) collective-permute-start(f32[2,256]{1,0:T(2,128)} %shard_map.46), channel_id=1, source_target_pairs={{0,2},{2,0},{4,6},{6,4},{8,10},{10,8},{12,14},{14,12},{16,18},{18,... | collective-permute-start | bytes 6152 | tf_op jit(solution)/shard_map/ppermute | solution.py:502
  12.2 19.9 %collective-permute-start.1 = (f32[2,2,128,512]{3,2,1,0:T(8,128)S(1)}, f32[2,2,128,512]{3,2,1,0:T(8,128)S(1)}, u32[]{:S(2)}, u32[]{:S(2)}) collective-permute-start(f32[2,2,128,512]{3,2,1,0:T(8,128)S(1)} %get-tuple-element.40), channel_id=1, source_target_pairs={{0,2},{2,0},{4,6},{6,4},{8,10},{10,8},{12,14},{14,12},{16,18},{18,... | collective-permute-start | bytes 3145736 | tf_op jit(solution)/shard_map/ppermute | solution.py:502
  12.6 25.1 %collective-permute-start.9 = (f32[2,2,128,512]{3,2,1,0:T(8,128)S(1)}, f32[2,2,128,512]{3,2,1,0:T(8,128)S(1)}, u32[]{:S(2)}, u32[]{:S(2)}) collective-permute-start(f32[2,2,128,512]{3,2,1,0:T(8,128)S(1)} %get-tuple-element.56), channel_id=1, source_target_pairs={{0,2},{2,0},{4,6},{6,4},{8,10},{10,8},{12,14},{14,12},{16,18},{18,... | collective-permute-start | bytes 3145736 | tf_op jit(solution)/shard_map/ppermute | solution.py:502
  12.8 3.9 %collective-permute-start.2 = (f32[2,256]{1,0:T(2,128)S(1)}, f32[2,256]{1,0:T(2,128)S(1)}, u32[]{:S(2)}, u32[]{:S(2)}) collective-permute-start(f32[2,256]{1,0:T(2,128)S(1)} %add.27.refs_4_), channel_id=1, source_target_pairs={{0,1},{1,0},{2,3},{3,2},{4,5},{5,4},{6,7},{7,6},{8,9},{9,8},{10,11... | collective-permute-start | bytes 6152 | tf_op jit(solution)/shard_map/ppermute | solution.py:538
  18.3 13.7 %collective-permute-start.3 = (f32[2,128,512]{2,1,0:T(8,128)S(1)}, f32[2,128,512]{2,1,0:T(8,128)S(1)}, u32[]{:S(2)}, u32[]{:S(2)}) collective-permute-start(f32[2,128,512]{2,1,0:T(8,128)S(1)} %get-tuple-element.42), channel_id=1, source_target_pairs={{0,252},{2,6},{4,0},{6,10},{8,4},{10,14},{12,8},{14,18},{16,12},{1... | collective-permute-start | bytes 1572872 | tf_op jit(solution)/shard_map/ppermute | solution.py:502
  18.4 19.3 %collective-permute-start.10 = (f32[2,128,512]{2,1,0:T(8,128)S(1)}, f32[2,128,512]{2,1,0:T(8,128)S(1)}, u32[]{:S(2)}, u32[]{:S(2)}) collective-permute-start(f32[2,128,512]{2,1,0:T(8,128)S(1)} %get-tuple-element.57), channel_id=1, source_target_pairs={{0,252},{2,6},{4,0},{6,10},{8,4},{10,14},{12,8},{14,18},{16,12},{1... | collective-permute-start | bytes 1572872 | tf_op jit(solution)/shard_map/ppermute | solution.py:502
  19.0 2.5 %collective-permute-start.4 = (f32[4,256]{1,0:T(4,128)S(1)}, f32[4,256]{1,0:T(4,128)S(1)}, u32[]{:S(2)}, u32[]{:S(2)}) collective-permute-start(f32[4,256]{1,0:T(4,128)S(1)} %maximum_add_fusion.refs_4_), channel_id=1, source_target_pairs={{0,32},{2,34},{4,36},{6,38},{8,40},{10,42},{12,44},{14,46},{16,48}... | collective-permute-start | bytes 12296 | tf_op jit(solution)/shard_map/ppermute | solution.py:502
  21.5 5.8 %collective-permute-start.5 = (f32[4,256]{1,0:T(4,128)S(1)}, f32[4,256]{1,0:T(4,128)S(1)}, u32[]{:S(2)}, u32[]{:S(2)}) collective-permute-start(f32[4,256]{1,0:T(4,128)S(1)} %add.29.refs_0_), channel_id=1, source_target_pairs={{0,64},{2,66},{4,68},{6,70},{8,72},{10,74},{12,76},{14,78},{16,80}... | collective-permute-start | bytes 12296 | tf_op jit(solution)/shard_map/ppermute | solution.py:502
  32.3 10.7 %collective-permute-start.6 = (f32[2,136,512]{2,1,0:T(8,128)S(1)}, f32[2,136,512]{2,1,0:T(8,128)S(1)}, u32[]{:S(2)}, u32[]{:S(2)}) collective-permute-start(f32[2,136,512]{2,1,0:T(8,128)S(1)} %get-tuple-element.44.refs_2_), channel_id=1, source_target_pairs={{0,254},{2,4},{4,2},{6,8},{8,6},{10,12},{12,10},{14,16},{16,14},{1... | collective-permute-start | bytes 1671176 | tf_op jit(solution)/shard_map/ppermute | solution.py:502
  37.9 17.9 %collective-permute-start.11 = (f32[2,136,512]{2,1,0:T(8,128)S(1)}, f32[2,136,512]{2,1,0:T(8,128)S(1)}, u32[]{:S(2)}, u32[]{:S(2)}) collective-permute-start(f32[2,136,512]{2,1,0:T(8,128)S(1)} %get-tuple-element.59.refs_2_), channel_id=1, source_target_pairs={{0,254},{2,4},{4,2},{6,8},{8,6},{10,12},{12,10},{14,16},{16,14},{1... | collective-permute-start | bytes 1671176 | tf_op jit(solution)/shard_map/ppermute | solution.py:502
  38.0 4.3 %collective-permute-start.7 = (f32[4,256]{1,0:T(4,128)S(1)}, f32[4,256]{1,0:T(4,128)S(1)}, u32[]{:S(2)}, u32[]{:S(2)}) collective-permute-start(f32[4,256]{1,0:T(4,128)S(1)} %add.30.refs_4_), channel_id=1, source_target_pairs={{0,128},{2,130},{4,132},{6,134},{8,136},{10,138},{12,140},{14,142}... | collective-permute-start | bytes 12296 | tf_op jit(solution)/shard_map/ppermute | solution.py:502
  43.2 7.3 %collective-permute-start.8 = (f32[2,8,512]{2,1,0:T(8,128)S(1)}, f32[2,8,512]{2,1,0:T(8,128)S(1)}, u32[]{:S(2)}, u32[]{:S(2)}) collective-permute-start(f32[2,8,512]{2,1,0:T(8,128)S(1)} %get-tuple-element.48), channel_id=1, source_target_pairs={{0,2},{2,0},{4,6},{6,4},{8,10},{10,8},{12,14},{14,12},{16,18},{18,... | collective-permute-start | bytes 98312 | tf_op jit(solution)/shard_map/ppermute | solution.py:502
  49.7 6.1 %collective-permute-start.12 = (f32[4,256]{1,0:T(4,128)S(1)}, f32[4,256]{1,0:T(4,128)S(1)}, u32[]{:S(2)}, u32[]{:S(2)}) collective-permute-start(f32[4,256]{1,0:T(4,128)S(1)} %add_add_fusion.refs_3_), channel_id=1, source_target_pairs={{0,4},{2,6},{4,0},{6,2},{8,12},{10,14},{12,8},{14,10},{16,20},{18,... | collective-permute-start | bytes 12296 | tf_op jit(solution)/shard_map/ppermute | solution.py:502
  50.8 9.4 %collective-permute-start.14 = (f32[2,32,768]{2,1,0:T(8,128)S(1)}, f32[2,32,768]{2,1,0:T(8,128)S(1)}, u32[]{:S(2)}, u32[]{:S(2)}) collective-permute-start(f32[2,32,768]{2,1,0:T(8,128)S(1)} %get-tuple-element.63), channel_id=1, source_target_pairs={{0,1},{1,0},{2,3},{3,2},{4,5},{5,4},{6,7},{7,6},{8,9},{9,8},{10,11... | collective-permute-start | bytes 589832 | tf_op jit(solution)/shard_map/ppermute | solution.py:588
  56.0 4.1 %collective-permute-start.13 = (f32[2,8,512]{2,1,0:T(8,128)S(1)}, f32[2,8,512]{2,1,0:T(8,128)S(1)}, u32[]{:S(2)}, u32[]{:S(2)}) collective-permute-start(f32[2,8,512]{2,1,0:T(8,128)S(1)} %get-tuple-element.62), channel_id=1, source_target_pairs={{0,2},{2,0},{4,6},{6,4},{8,10},{10,8},{12,14},{14,12},{16,18},{18,... | collective-permute-start | bytes 98312 | tf_op jit(solution)/shard_map/ppermute | solution.py:502
  56.7 3.4 %collective-permute-start.15 = (f32[4,256]{1,0:T(4,128)S(1)}, f32[4,256]{1,0:T(4,128)S(1)}, u32[]{:S(2)}, u32[]{:S(2)}) collective-permute-start(f32[4,256]{1,0:T(4,128)S(1)} %get-tuple-element.71), channel_id=1, source_target_pairs={{0,8},{2,10},{4,12},{6,14},{8,0},{10,2},{12,4},{14,6},{16,24},{18,... | collective-permute-start | bytes 12296 | tf_op jit(solution)/shard_map/ppermute | solution.py:502
  60.1 6.4 %collective-permute-start.16 = (f32[4,256]{1,0:T(4,128)S(1)}, f32[4,256]{1,0:T(4,128)S(1)}, u32[]{:S(2)}, u32[]{:S(2)}) collective-permute-start(f32[4,256]{1,0:T(4,128)S(1)} %add.35.refs_4_), channel_id=1, source_target_pairs={{0,16},{2,18},{4,20},{6,22},{8,24},{10,26},{12,28},{14,30},{16,0},... | collective-permute-start | bytes 12296 | tf_op jit(solution)/shard_map/ppermute | solution.py:502

commit v2 on v1

--- a/solution.py
+++ b/solution.py
@@ -102,26 +102,44 @@
             sums[f : f + 1, 128 * j : 128 * j + 128] = jnp.sum(block, axis=0, keepdims=True)
 
 
-def far_kernel(cols_hbm, count_hbm, cbuf, ebuf, near_out, far_out, cols, count, ssem):
+def far_kernel(cols_hbm, count_hbm, c_hbm, e_hbm, out, cols, count, cbuf, ebuf, ssem, sem):
     lon, core, lat = where_am_i()
     scalars = fetch_scalars(cols_hbm, count_hbm, cols, count, ssem)
     wanted = jnp.where(core == 1, 1, -2)
-    near_out[...] = jnp.zeros(near_out.shape, F32)
-    far_out[...] = jnp.zeros(far_out.shape, F32)
     for copy in scalars:
         copy.wait()
+
+    def need(slot):
+        return jnp.logical_and(slot < count[0], slot_place(cols, slot, lon)[1] == wanted)
+
+    def loads(slot):
+        return (
+            pltpu.make_async_copy(c_hbm.at[slot], cbuf.at[slot], sem.at[0, slot]),
+            pltpu.make_async_copy(e_hbm.at[slot], ebuf.at[slot], sem.at[1, slot]),
+        )
+
     for slot in range(4):
-        within, rel = slot_place(cols, slot, lon)
-
-        @pl.when(jnp.logical_and(slot < count[0], rel == wanted))
-        def _(slot=slot, within=within):
+
+        @pl.when(need(slot))
+        def _(slot=slot):
+            for load in loads(slot):
+                load.start()
+
+    out[...] = jnp.zeros(out.shape, F32)
+    for slot in range(4):
+
+        @pl.when(need(slot))
+        def _(slot=slot):
+            for load in loads(slot):
+                load.wait()
+            within, _ = slot_place(cols, slot, lon)
             lane = iota((8, 128), 1)
 
-            for out, start in ((near_out, HALF * (1 - lat)), (far_out, HALF * lat)):
-
-                def body(g, carry, out=out, start=start):
+            for first, start in ((0, HALF * (1 - lat)), (HALF, HALF * lat)):
+
+                def body(g, carry, first=first, start=start):
                     rows = pl.ds(pl.multiple_of(start + 8 * g, 8), 8)
-                    here = pl.ds(pl.multiple_of(8 * g, 8), 8)
+                    here = pl.ds(pl.multiple_of(first + 8 * g, 8), 8)
                     for f, buf in ((0, cbuf), (1, ebuf)):
                         x = rolled(buf, slot, rows, within)
                         for j in range(4):
@@ -183,11 +201,15 @@
         lax.fori_loop(0, HALF // 8, body, 0, unroll=4)
 
 
-def merge_kernel(q1, q0, a, b1, partial, message):
+def token_kernel(arrived, token):
+    token[...] = jnp.zeros(token.shape, F32)
+
+
+def merge_kernel(first, q1, q0, a, b1, partial, message):
     _, core, _ = where_am_i()
     for f in range(2):
         message[f, :HALF, :] = q1[f] + a[1, f]
-        mine = q0[f] + a[0, f] + b1[f]
+        mine = q0[f] + a[0, f] + b1[f, first : first + HALF, :]
         partial[f] = mine
         edge = jnp.where(core == 1, pltpu.roll(mine[:, 384:], 32, 1), mine[:, :128])
         message[f, HALF:, :] = pack(edge)
@@ -415,14 +437,11 @@
     waves = (far_wave, near_wave)
     varis = (far_vari, near_vari)
 
-    for s in range(SCALES):
+    def prepare(s):
         factor = [1.0 / (table[s][0] * table[s][2]), 1.0 / table[s][1] ** 2]
         factor.append(factor[0])
-        slot = s % 2
-        for parts, span, w, v, tap, var, start in (
-            (far_parts, FAR_K, fw, fv, far_tap, far_var, HALF * lat),
-            (near_parts, NEAR_K, nw, nv, near_tap, near_var, HALF * (1 - lat)),
-        ):
+        slot = s
+        for parts, span, w, v in ((far_parts, FAR_K, fw, fv), (near_parts, NEAR_K, nw, nv)):
             for source, rows, which, rrows, at in parts:
                 size = HALF if at == 0 else RAD
                 r = rate[which, rrows, :]
@@ -439,11 +458,28 @@
                         for copy, t in enumerate(split(t)):
                             first = span * (3 * copy + k) + at
                             v[slot, first : first + size, cols] = t
+
+    def multiply(s):
+        slot = s
+        for w, v, tap, var, start in (
+            (fw, fv, far_tap, far_var, HALF * lat),
+            (nw, nv, near_tap, near_var, HALF * (1 - lat)),
+        ):
             wavelet = mm(tap[s], w[slot])
             variance = mm(var[s], v[slot])
             signal = wavelet * lax.rsqrt(jnp.maximum(variance, 1.0))
             there = pl.ds(pl.multiple_of(start, HALF), HALF)
             out[s, there, :] = pltpu.roll(signal, 64, 1)
+
+    @pl.when(lat >= 0)
+    def _():
+        for s in range(SCALES):
+            prepare(s)
+
+    @pl.when(lat >= 0)
+    def _():
+        for s in range(SCALES):
+            multiply(s)
 
 
 VMEM = pl.BlockSpec(memory_space=pltpu.VMEM)
@@ -482,7 +518,7 @@
     ((SCALES, HALF, 6 * NEAR_K), BF16),
 ]
 FINAL_SCRATCH = [pltpu.VMEM((3, HALF, 128), F32)] + [
-    pltpu.VMEM((2, 6 * span, TW), BF16) for span in (FAR_K, FAR_K, NEAR_K, NEAR_K)
+    pltpu.VMEM((SCALES, 6 * span, TW), BF16) for span in (FAR_K, FAR_K, NEAR_K, NEAR_K)
 ]
 
 
@@ -537,32 +573,31 @@
     af = on_lon(af, partner)
     other = lax.ppermute(sums, "lat", [(0, 1), (1, 0)])
     sums = jnp.concatenate([sums, other], axis=0) + rest_token
-    far_n, far_f = call(
+    (b1,) = call(
         far_kernel,
-        [(piece, F32), (piece, F32)],
-        [ANY, ANY, VMEM, VMEM],
-        scalars + semaphores[:1],
-        after=[sums],
-        us=1.5,
-        limit=24,
+        [((2, 2 * HALF, TW), F32)],
+        [ANY] * 4,
+        scalars + [pltpu.VMEM(blocks, jnp.int32), pltpu.VMEM(blocks, F32)] + semaphores,
+        limit=58,
     )(*inputs)
-    b1_n = on_lon(far_n, two_out)
-    b1_f = on_lon(far_f, two_out)
+    b1 = on_lon(b1, two_out)
     steps = [sums]
+    (b1_token,) = call(token_kernel, [(TOKEN, F32)], [ANY])(b1)
     sums = sums + on_lon(sums, lambda i: i ^ 16)
-    steps.append(sums)
+    steps.append(sums + b1_token)
     ctap, cvar, far_tap, near_tap, far_var, near_var, taps_token = call(
         taps_kernel, TAPS + [(TOKEN, F32)], [], after=[steps[1]], us=3.0
     )()
+    sums = steps[1]
     for flip in (32, 64, 2):
         sums = sums + on_lon(sums, lambda i: i ^ flip)
         if flip == 64:
             sums = sums + taps_token
         steps.append(sums)
 
-    def merge(after, *pieces):
+    def merge(first, after, *pieces):
         return call(
-            merge_kernel,
+            functools.partial(merge_kernel, first),
             [(piece, F32), ((2, HALF + 8, TW), F32)],
             [VMEM] * 4,
             after=after,
@@ -576,9 +611,9 @@
             after=after,
         )(*pieces)
 
-    partial_n, sent_n = merge([steps[2]], q1n, q0n, an, b1_n)
+    partial_n, sent_n = merge(0, [steps[1]], q1n, q0n, an, b1)
     b2_n = on_lon(sent_n, one_out)
-    partial_f, sent_f = merge([steps[2]], q1f, q0f, af, b1_f)
+    partial_f, sent_f = merge(HALF, [steps[1]], q1f, q0f, af, b1)
     b2_f = on_lon(sent_f, one_out)
     total_n, outer_n, inner_n = totals([steps[3]], partial_n, b2_n, sent_n)
     inner_n = on_lon(inner_n, partner)

time: 72.8 us -> 71.5 us (0.982)
  waiting for transfers between devices: 21.6 us -> 15.3 us
  starting transfers between devices: 25.6 us -> 28.8 us
  Pallas kernels: 23.7 us -> 25.4 us
    ppermute x15 -> x14, waiting for transfers between devices: 18.9 us -> 13.9 us  [on_lon(): return lax.ppermute(value, 'lon', [(i, step(i) % LON) for i in range(LON)])]
    ppermute x15 -> x14, starting transfers between devices: 21.7 us -> 23.4 us  [on_lon(): return lax.ppermute(value, 'lon', [(i, step(i) % LON) for i in range(LON)])]
    pallas_call x12 -> x13, Pallas kernels: 23.7 us -> 25.4 us  [run(): pl.pallas_call(body, out_shape=[jax.ShapeDtypeStruct(shape, dtype) for sh...]
    ppermute x1, starting transfers between devices: 1.18 us -> 2.62 us  [per_device(): other = lax.ppermute(sums, 'lat', [(0, 1), (1, 0)])]
    ppermute x1, waiting for transfers between devices: 2.76 us -> 1.32 us  [per_device(): other = lax.ppermute(sums, 'lat', [(0, 1), (1, 0)])]
  transfers between devices with their start and end apart: 17 -> 16, of which waited for: 10 -> 9; matrix products, arithmetic and copies ran while one was open for 0% -> 1% of each run, Pallas kernels for 15% -> 22%
where the time goes in v2:
time: 71.5 us; the launch traced here: 71 us
  starting transfers between devices  28.8 us (40%)
  Pallas kernels  25.4 us (36%)
  waiting for transfers between devices  15.3 us (21%)
  between operations  0.84 us (1%)
    pallas_call x13, Pallas kernels, run(): pl.pallas_call(body, out_shape=[jax.ShapeDtypeStruct(shape, dtype) for sh...  25.4 us
    ppermute x14, starting transfers between devices, on_lon(): return lax.ppermute(value, 'lon', [(i, step(i) % LON) for i in range(LON)])  23.4 us
    ppermute x14, waiting for transfers between devices, on_lon(): return lax.ppermute(value, 'lon', [(i, step(i) % LON) for i in range(LON)])  13.9 us
    ppermute x1, starting transfers between devices, per_device(): lat_rows = lax.ppermute(message, 'lat', [(0, 1), (1, 0)])  2.71 us
    ppermute x1, starting transfers between devices, per_device(): other = lax.ppermute(sums, 'lat', [(0, 1), (1, 0)])  2.62 us
  transfers between devices with their start and end apart: 16, of which 9 were waited for; matrix products, arithmetic and copies ran while one was open for 1% of the time, Pallas kernels for 22%

profile of v2, /device:TPU:1, one launch (start us, length us, event | category | flops | bytes accessed | tf_op | source)
XLA Modules:
  0.0 71.0 jit_solution(12184222245449153357)
XLA Ops:
  0.7 3.9 %shard_map.48 = f32[2,256,512]{2,1,0:T(8,128)} custom-call(s32[4]{0:T(128)} %refs_0_.4, s32[1]{0:T(128)S(6)} %copy.5.refs_0_.refs_1_, s32[4,256,512]{2,1,0:T(8,128)} %refs_2_.5, f32[4,256,512]{2,1,0:T(8,128)} %refs_3_.3), custom_call_target="tpu_custom_call" | custom-call | bytes 36000 | tf_op jit(solution)/shard_map/pallas_call | solution.py:496
  4.5 0.0 copy-start
  4.6 0.0 copy-start.1
  4.6 0.0 copy-start.2
  4.6 0.5 collective-permute-start.2
  5.1 3.2 %shard_map.46 = f32[2,256]{1,0:T(2,128)} custom-call(s32[1]{0:T(128)S(6)} %copy.5.refs_0_.refs_1_, s32[4,256,512]{2,1,0:T(8,128)} %refs_2_.5, f32[4,256,512]{2,1,0:T(8,128)} %refs_3_.3), custom_call_target="tpu_custom_call" | custom-call | bytes 36000 | tf_op jit(solution)/shard_map/pallas_call | solution.py:496
  8.3 10.0 %collective-permute-start = (f32[2,256]{1,0:T(2,128)}, f32[2,256]{1,0:T(2,128)S(1)}, u32[]{:S(2)}, u32[]{:S(2)}) collective-permute-start(f32[2,256]{1,0:T(2,128)} %shard_map.46), channel_id=1, source_target_pairs={{0,2},{2,0},{4,6},{6,4},{8,10},{10,8},{12,14},{14,12},{16,18},{18,... | collective-permute-start | bytes 6152 | tf_op jit(solution)/shard_map/ppermute | solution.py:538
  18.3 1.0 %collective-permute-done = f32[2,256]{1,0:T(2,128)S(1)} collective-permute-done((f32[2,256]{1,0:T(2,128)}, f32[2,256]{1,0:T(2,128)S(1)}, u32[]{:S(2)}, u32[]{:S(2)}) %collective-permute-start) | collective-permute-done | bytes 2080 | tf_op jit(solution)/shard_map/ppermute | solution.py:538
  19.4 0.7 add.30.refs_4_
  20.1 0.0 copy-done
  20.1 0.0 copy-done.1
  20.1 0.0 copy-done.2
  20.1 2.9 %shard_map.47 = (f32[2,128,512]{2,1,0:T(8,128)S(1)}, f32[2,128,512]{2,1,0:T(8,128)S(1)}, f32[2,128,512]{2,1,0:T(8,128)S(1)}, f32[2,128,512]{2,1,0:T(8,128)S(1)},...) custom-call(s32[4]{0:T(128)S(1)} %copy-done.2, s32[1]{0:T(128)S(6)} %copy.5.refs_0_.refs_1_, ...), custom_call_target="tpu_custom_call" | custom-call | bytes 10800000 | tf_op jit(solution)/shard_map/pallas_call | solution.py:496
  23.0 0.4 collective-permute-start.1
  23.4 0.2 collective-permute-start.9
  23.6 2.6 %collective-permute-start.3 = (f32[2,256]{1,0:T(2,128)S(1)}, f32[2,256]{1,0:T(2,128)S(1)}, u32[]{:S(2)}, u32[]{:S(2)}) collective-permute-start(f32[2,256]{1,0:T(2,128)S(1)} %add.30.refs_4_), channel_id=1, source_target_pairs={{0,1},{1,0},{2,3},{3,2},{4,5},{5,4},{6,7},{7,6},{8,9},{9,8},{10,11... | collective-permute-start | bytes 6152 | tf_op jit(solution)/shard_map/ppermute | solution.py:574
  26.2 1.3 %collective-permute-done.3 = f32[2,256]{1,0:T(2,128)S(1)} collective-permute-done((f32[2,256]{1,0:T(2,128)S(1)}, f32[2,256]{1,0:T(2,128)S(1)}, u32[]{:S(2)}, u32[]{:S(2)}) %collective-permute-start.3) | collective-permute-done | bytes 2080 | tf_op jit(solution)/shard_map/ppermute | solution.py:574
  27.6 0.1 collective-permute-start.4
  27.7 0.8 %collective-permute-done.2.refs_0_.refs_3_ = f32[2,256,512]{2,1,0:T(8,128)S(1)} collective-permute-done((f32[2,256,512]{2,1,0:T(8,128)}, f32[2,256,512]{2,1,0:T(8,128)S(1)}, u32[]{:S(2)}, u32[]{:S(2)}) %collective-permute-start.2) | collective-permute-done | bytes 1048608 | tf_op jit(solution)/shard_map/ppermute | solution.py:538
  28.5 1.6 %collective-permute-done.4 = f32[4,256]{1,0:T(4,128)S(1)} collective-permute-done((f32[4,256]{1,0:T(4,128)S(1)}, f32[4,256]{1,0:T(4,128)S(1)}, u32[]{:S(2)}, u32[]{:S(2)}) %collective-permute-start.4) | collective-permute-done | bytes 4128 | tf_op jit(solution)/shard_map/ppermute | solution.py:538
  30.1 0.0 collective-permute-done.1.refs_2_
  30.1 0.2 shard_map.50
  30.3 0.1 collective-permute-start.5
  30.4 0.0 collective-permute-done.9.refs_2_
  30.4 0.2 shard_map.55
  30.7 1.8 %collective-permute-start.10 = (f32[2,136,512]{2,1,0:T(8,128)S(1)}, f32[2,136,512]{2,1,0:T(8,128)S(1)}, u32[]{:S(2)}, u32[]{:S(2)}) collective-permute-start(f32[2,136,512]{2,1,0:T(8,128)S(1)} %get-tuple-element.55.refs_2_), channel_id=1, source_target_pairs={{0,254},{2,4},{4,2},{6,8},{8,6},{10,12},{12,10},{14,16},{16,14},{1... | collective-permute-start | bytes 1671176 | tf_op jit(solution)/shard_map/ppermute | solution.py:538
  32.5 0.0 collective-permute-start.6
  32.5 2.5 %collective-permute-done.6 = f32[4,256]{1,0:T(4,128)S(1)} collective-permute-done((f32[4,256]{1,0:T(4,128)S(1)}, f32[4,256]{1,0:T(4,128)S(1)}, u32[]{:S(2)}, u32[]{:S(2)}) %collective-permute-start.6) | collective-permute-done | bytes 4128 | tf_op jit(solution)/shard_map/ppermute | solution.py:538
  34.9 0.7 collective-permute-start.7
  35.6 3.5 %shard_map.51 = (bf16[2,768,768]{2,1,0:T(8,128)(2,1)S(1)}, bf16[2,512,1152]{2,1,0:T(8,128)(2,1)S(1)}, bf16[3,128,960]{2,1,0:T(8,128)(2,1)S(1)}, bf16[3,128,1152]...) custom-call(f32[4,256]{1,0:T(4,128)S(1)} %add_add_fusion.1.refs_4_.r, ...), custom_call_target="tpu_custom_call" | custom-call | bytes 10800000 | tf_op jit(solution)/shard_map/pallas_call | solution.py:496
  39.1 0.0 collective-permute-done.7
  39.2 0.2 collective-permute-done.5.refs_1_
  39.4 0.2 shard_map.52
  39.6 8.9 %collective-permute-start.8 = (f32[2,8,512]{2,1,0:T(8,128)S(1)}, f32[2,8,512]{2,1,0:T(8,128)S(1)}, u32[]{:S(2)}, u32[]{:S(2)}) collective-permute-start(f32[2,8,512]{2,1,0:T(8,128)S(1)} %get-tuple-element.45), channel_id=1, source_target_pairs={{0,2},{2,0},{4,6},{6,4},{8,10},{10,8},{12,14},{14,12},{16,18},{18,... | collective-permute-start | bytes 98312 | tf_op jit(solution)/shard_map/ppermute | solution.py:538
  48.6 0.0 collective-permute-start.11
  48.6 0.9 %collective-permute-done.8.refs_2_ = f32[2,8,512]{2,1,0:T(8,128)S(1)} collective-permute-done((f32[2,8,512]{2,1,0:T(8,128)S(1)}, f32[2,8,512]{2,1,0:T(8,128)S(1)}, u32[]{:S(2)}, u32[]{:S(2)}) %collective-permute-start.8) | collective-permute-done | bytes 32800 | tf_op jit(solution)/shard_map/ppermute | solution.py:538
  49.4 0.2 shard_map.53
  49.6 2.7 %collective-permute-start.13 = (f32[2,32,768]{2,1,0:T(8,128)S(1)}, f32[2,32,768]{2,1,0:T(8,128)S(1)}, u32[]{:S(2)}, u32[]{:S(2)}) collective-permute-start(f32[2,32,768]{2,1,0:T(8,128)S(1)} %get-tuple-element.59), channel_id=1, source_target_pairs={{0,1},{1,0},{2,3},{3,2},{4,5},{5,4},{6,7},{7,6},{8,9},{9,8},{10,11... | collective-permute-start | bytes 589832 | tf_op jit(solution)/shard_map/ppermute | solution.py:623
  52.4 2.3 %shard_map.54 = (f32[3,4,128,512]{3,2,1,0:T(8,128)S(1)}, f32[3,3,128,512]{3,2,1,0:T(8,128)S(1)}, f32[4,256]{1,0:T(4,128)S(1)}) custom-call(f32[2,128,512]{2,1,0:T(8,128)S(1)} %get-tuple-element.43.refs_0_, f32[2,128,256]{2,1,0:T(8,128)S(1)} %get-tuple-element.46.refs_1_, bf16[2,768,768]{2,1,0:T(8,128)(2,1)S(1)} %get-tuple-element.47.refs_2_.refs_4_, ...), custom_call_target="tpu_custom_call" | custom-call | bytes 14400000 | tf_op jit(solution)/shard_map/pallas_call | solution.py:496
  54.6 0.0 collective-permute-done.11
  54.6 0.0 collective-permute-done.10.refs_1_
  54.7 0.2 shard_map.56
  54.9 0.7 %collective-permute-start.12 = (f32[2,8,512]{2,1,0:T(8,128)S(1)}, f32[2,8,512]{2,1,0:T(8,128)S(1)}, u32[]{:S(2)}, u32[]{:S(2)}) collective-permute-start(f32[2,8,512]{2,1,0:T(8,128)S(1)} %get-tuple-element.58), channel_id=1, source_target_pairs={{0,2},{2,0},{4,6},{6,4},{8,10},{10,8},{12,14},{14,12},{16,18},{18,... | collective-permute-start | bytes 98312 | tf_op jit(solution)/shard_map/ppermute | solution.py:538
  55.6 0.0 collective-permute-start.14
  55.6 3.4 %collective-permute-done.14 = f32[4,256]{1,0:T(4,128)S(1)} collective-permute-done((f32[4,256]{1,0:T(4,128)S(1)}, f32[4,256]{1,0:T(4,128)S(1)}, u32[]{:S(2)}, u32[]{:S(2)}) %collective-permute-start.14) | collective-permute-done | bytes 4128 | tf_op jit(solution)/shard_map/ppermute | solution.py:538
  59.0 0.0 collective-permute-start.15
  59.0 0.0 collective-permute-done.12.refs_2_
  59.0 0.0 collective-permute-done.13.refs_3_
  59.0 2.8 %shard_map.57 = (f32[3,4,160,512]{3,2,1,0:T(8,128)S(1)}, f32[3,3,160,512]{3,2,1,0:T(8,128)S(1)}) custom-call(f32[2,128,512]{2,1,0:T(8,128)S(1)} %get-tuple-element.56.refs_0_, f32[2,128,128]{2,1,0:T(8,128)S(1)} %get-tuple-element.57.refs_1_, f32[2,8,512]{2,1,0:T(8,128)S(1)} %collective-permute-done.12.refs_2_, ...), custom_call_target="tpu_custom_call" | custom-call | bytes 18000000 | tf_op jit(solution)/shard_map/pallas_call | solution.py:496
  61.8 3.6 %collective-permute-done.15.refs_5_ = f32[4,256]{1,0:T(4,128)S(1)} collective-permute-done((f32[4,256]{1,0:T(4,128)S(1)}, f32[4,256]{1,0:T(4,128)S(1)}, u32[]{:S(2)}, u32[]{:S(2)}) %collective-permute-start.15) | collective-permute-done | bytes 4128 | tf_op jit(solution)/shard_map/ppermute | solution.py:538
  65.4 5.6 %shard_map.58 = f32[3,256,512]{2,1,0:T(8,128)} custom-call(f32[3,4,128,512]{3,2,1,0:T(8,128)S(1)} %get-tuple-element.49.refs_0_, f32[3,3,128,512]{3,2,1,0:T(8,128)S(1)} %get-tuple-element.50.refs_1_, f32[3,4,160,512]{3,2,1,0:T(8,128)S(1)} %get-tuple-element.60.refs_2_, f32[3,3,160,512]{3,2,1,0:T(8,128)S(1)} %get-tuple-element.61.refs_3_, ...), custom_call_target="tpu_custom_call" | custom-call | bytes 36000 | tf_op jit(solution)/shard_map/pallas_call | solution.py:496
  (7 shorter events, 0.0 us)
Async XLA Ops:
  4.5 15.5 %copy-start = (s32[4,256,512]{2,1,0:T(8,128)S(1)}, s32[4,256,512]{2,1,0:T(8,128)}, u32[]{:S(2)}) copy-start(s32[4,256,512]{2,1,0:T(8,128)} %refs_2_.5) | copy-start | bytes 6291460
  4.6 15.5 %copy-start.1 = (f32[4,256,512]{2,1,0:T(8,128)S(1)}, f32[4,256,512]{2,1,0:T(8,128)}, u32[]{:S(2)}) copy-start(f32[4,256,512]{2,1,0:T(8,128)} %refs_3_.3) | copy-start | bytes 6291460
  4.6 15.5 %copy-start.2 = (s32[4]{0:T(128)S(1)}, s32[4]{0:T(128)}, u32[]{:S(2)}) copy-start(s32[4]{0:T(128)} %refs_0_.4) | copy-start | bytes 52
  4.6 23.9 %collective-permute-start.2 = (f32[2,256,512]{2,1,0:T(8,128)}, f32[2,256,512]{2,1,0:T(8,128)S(1)}, u32[]{:S(2)}, u32[]{:S(2)}) collective-permute-start(f32[2,256,512]{2,1,0:T(8,128)} %shard_map.48), channel_id=1, source_target_pairs={{0,252},{2,6},{4,0},{6,10},{8,4},{10,14},{12,8},{14,18},{16,12},{1... | collective-permute-start | bytes 3145736 | tf_op jit(solution)/shard_map/ppermute | solution.py:538
  8.3 11.0 %collective-permute-start = (f32[2,256]{1,0:T(2,128)}, f32[2,256]{1,0:T(2,128)S(1)}, u32[]{:S(2)}, u32[]{:S(2)}) collective-permute-start(f32[2,256]{1,0:T(2,128)} %shard_map.46), channel_id=1, source_target_pairs={{0,2},{2,0},{4,6},{6,4},{8,10},{10,8},{12,14},{14,12},{16,18},{18,... | collective-permute-start | bytes 6152 | tf_op jit(solution)/shard_map/ppermute | solution.py:538
  23.0 7.1 %collective-permute-start.1 = (f32[2,2,128,512]{3,2,1,0:T(8,128)S(1)}, f32[2,2,128,512]{3,2,1,0:T(8,128)S(1)}, u32[]{:S(2)}, u32[]{:S(2)}) collective-permute-start(f32[2,2,128,512]{3,2,1,0:T(8,128)S(1)} %get-tuple-element.38), channel_id=1, source_target_pairs={{0,2},{2,0},{4,6},{6,4},{8,10},{10,8},{12,14},{14,12},{16,18},{18,... | collective-permute-start | bytes 3145736 | tf_op jit(solution)/shard_map/ppermute | solution.py:538
  23.4 7.0 %collective-permute-start.9 = (f32[2,2,128,512]{3,2,1,0:T(8,128)S(1)}, f32[2,2,128,512]{3,2,1,0:T(8,128)S(1)}, u32[]{:S(2)}, u32[]{:S(2)}) collective-permute-start(f32[2,2,128,512]{3,2,1,0:T(8,128)S(1)} %get-tuple-element.53), channel_id=1, source_target_pairs={{0,2},{2,0},{4,6},{6,4},{8,10},{10,8},{12,14},{14,12},{16,18},{18,... | collective-permute-start | bytes 3145736 | tf_op jit(solution)/shard_map/ppermute | solution.py:538
  23.6 3.9 %collective-permute-start.3 = (f32[2,256]{1,0:T(2,128)S(1)}, f32[2,256]{1,0:T(2,128)S(1)}, u32[]{:S(2)}, u32[]{:S(2)}) collective-permute-start(f32[2,256]{1,0:T(2,128)S(1)} %add.30.refs_4_), channel_id=1, source_target_pairs={{0,1},{1,0},{2,3},{3,2},{4,5},{5,4},{6,7},{7,6},{8,9},{9,8},{10,11... | collective-permute-start | bytes 6152 | tf_op jit(solution)/shard_map/ppermute | solution.py:574
  27.6 2.5 %collective-permute-start.4 = (f32[4,256]{1,0:T(4,128)S(1)}, f32[4,256]{1,0:T(4,128)S(1)}, u32[]{:S(2)}, u32[]{:S(2)}) collective-permute-start(f32[4,256]{1,0:T(4,128)S(1)} %maximum_add_fusion), channel_id=1, source_target_pairs={{0,32},{2,34},{4,36},{6,38},{8,40},{10,42},{12,44},{14,46},{16,48}... | collective-permute-start | bytes 12296 | tf_op jit(solution)/shard_map/ppermute | solution.py:538
  30.3 9.0 %collective-permute-start.5 = (f32[2,136,512]{2,1,0:T(8,128)S(1)}, f32[2,136,512]{2,1,0:T(8,128)S(1)}, u32[]{:S(2)}, u32[]{:S(2)}) collective-permute-start(f32[2,136,512]{2,1,0:T(8,128)S(1)} %get-tuple-element.41.refs_2_), channel_id=1, source_target_pairs={{0,254},{2,4},{4,2},{6,8},{8,6},{10,12},{12,10},{14,16},{16,14},{1... | collective-permute-start | bytes 1671176 | tf_op jit(solution)/shard_map/ppermute | solution.py:538
  30.7 24.0 %collective-permute-start.10 = (f32[2,136,512]{2,1,0:T(8,128)S(1)}, f32[2,136,512]{2,1,0:T(8,128)S(1)}, u32[]{:S(2)}, u32[]{:S(2)}) collective-permute-start(f32[2,136,512]{2,1,0:T(8,128)S(1)} %get-tuple-element.55.refs_2_), channel_id=1, source_target_pairs={{0,254},{2,4},{4,2},{6,8},{8,6},{10,12},{12,10},{14,16},{16,14},{1... | collective-permute-start | bytes 1671176 | tf_op jit(solution)/shard_map/ppermute | solution.py:538
  32.5 2.5 %collective-permute-start.6 = (f32[4,256]{1,0:T(4,128)S(1)}, f32[4,256]{1,0:T(4,128)S(1)}, u32[]{:S(2)}, u32[]{:S(2)}) collective-permute-start(f32[4,256]{1,0:T(4,128)S(1)} %add_add_fusion.1.refs_4_.refs_0_), channel_id=1, source_target_pairs={{0,64},{2,66},{4,68},{6,70},{8,72},{10,74},{12,76},{14,78},{16,80}... | collective-permute-start | bytes 12296 | tf_op jit(solution)/shard_map/ppermute | solution.py:538
  34.9 4.2 %collective-permute-start.7 = (f32[4,256]{1,0:T(4,128)S(1)}, f32[4,256]{1,0:T(4,128)S(1)}, u32[]{:S(2)}, u32[]{:S(2)}) collective-permute-start(f32[4,256]{1,0:T(4,128)S(1)} %add.34), channel_id=1, source_target_pairs={{0,128},{2,130},{4,132},{6,134},{8,136},{10,138},{12,140},{14,142}... | collective-permute-start | bytes 12296 | tf_op jit(solution)/shard_map/ppermute | solution.py:538
  39.6 9.8 %collective-permute-start.8 = (f32[2,8,512]{2,1,0:T(8,128)S(1)}, f32[2,8,512]{2,1,0:T(8,128)S(1)}, u32[]{:S(2)}, u32[]{:S(2)}) collective-permute-start(f32[2,8,512]{2,1,0:T(8,128)S(1)} %get-tuple-element.45), channel_id=1, source_target_pairs={{0,2},{2,0},{4,6},{6,4},{8,10},{10,8},{12,14},{14,12},{16,18},{18,... | collective-permute-start | bytes 98312 | tf_op jit(solution)/shard_map/ppermute | solution.py:538
  48.6 6.1 %collective-permute-start.11 = (f32[4,256]{1,0:T(4,128)S(1)}, f32[4,256]{1,0:T(4,128)S(1)}, u32[]{:S(2)}, u32[]{:S(2)}) collective-permute-start(f32[4,256]{1,0:T(4,128)S(1)} %add_add_fusion.refs_3_), channel_id=1, source_target_pairs={{0,4},{2,6},{4,0},{6,2},{8,12},{10,14},{12,8},{14,10},{16,20},{18,... | collective-permute-start | bytes 12296 | tf_op jit(solution)/shard_map/ppermute | solution.py:538
  49.6 9.4 %collective-permute-start.13 = (f32[2,32,768]{2,1,0:T(8,128)S(1)}, f32[2,32,768]{2,1,0:T(8,128)S(1)}, u32[]{:S(2)}, u32[]{:S(2)}) collective-permute-start(f32[2,32,768]{2,1,0:T(8,128)S(1)} %get-tuple-element.59), channel_id=1, source_target_pairs={{0,1},{1,0},{2,3},{3,2},{4,5},{5,4},{6,7},{7,6},{8,9},{9,8},{10,11... | collective-permute-start | bytes 589832 | tf_op jit(solution)/shard_map/ppermute | solution.py:623
  54.9 4.1 %collective-permute-start.12 = (f32[2,8,512]{2,1,0:T(8,128)S(1)}, f32[2,8,512]{2,1,0:T(8,128)S(1)}, u32[]{:S(2)}, u32[]{:S(2)}) collective-permute-start(f32[2,8,512]{2,1,0:T(8,128)S(1)} %get-tuple-element.58), channel_id=1, source_target_pairs={{0,2},{2,0},{4,6},{6,4},{8,10},{10,8},{12,14},{14,12},{16,18},{18,... | collective-permute-start | bytes 98312 | tf_op jit(solution)/shard_map/ppermute | solution.py:538
  55.6 3.4 %collective-permute-start.14 = (f32[4,256]{1,0:T(4,128)S(1)}, f32[4,256]{1,0:T(4,128)S(1)}, u32[]{:S(2)}, u32[]{:S(2)}) collective-permute-start(f32[4,256]{1,0:T(4,128)S(1)} %get-tuple-element.67), channel_id=1, source_target_pairs={{0,8},{2,10},{4,12},{6,14},{8,0},{10,2},{12,4},{14,6},{16,24},{18,... | collective-permute-start | bytes 12296 | tf_op jit(solution)/shard_map/ppermute | solution.py:538
  59.0 6.4 %collective-permute-start.15 = (f32[4,256]{1,0:T(4,128)S(1)}, f32[4,256]{1,0:T(4,128)S(1)}, u32[]{:S(2)}, u32[]{:S(2)}) collective-permute-start(f32[4,256]{1,0:T(4,128)S(1)} %add.39.refs_4_), channel_id=1, source_target_pairs={{0,16},{2,18},{4,20},{6,22},{8,24},{10,26},{12,28},{14,30},{16,0},... | collective-permute-start | bytes 12296 | tf_op jit(solution)/shard_map/ppermute | solution.py:538

commit v3 on v2

--- a/solution.py
+++ b/solution.py
@@ -69,17 +69,22 @@
     return copies
 
 
-def sums_kernel(count_hbm, c_hbm, e_hbm, sums, acc, count, cbuf, ebuf, ssem, sem):
-    scalar = pltpu.make_async_copy(count_hbm, count, ssem)
-    scalar.start()
+def first_kernel(
+    cols_hbm, count_hbm, c_hbm, e_hbm, out, sums, acc, cols, count, cbuf, ebuf, ssem, sem
+):
+    lon, core, lat = where_am_i()
+    scalars = fetch_scalars(cols_hbm, count_hbm, cols, count, ssem)
     copies = []
     for slot in range(4):
         copies.append(pltpu.make_async_copy(c_hbm.at[slot], cbuf.at[slot], sem.at[0, slot]))
         copies.append(pltpu.make_async_copy(e_hbm.at[slot], ebuf.at[slot], sem.at[1, slot]))
     for copy in copies:
         copy.start()
+    wanted = jnp.where(core == 1, 1, -2)
+    out[...] = jnp.zeros(out.shape, F32)
     acc[...] = jnp.zeros(acc.shape, F32)
-    scalar.wait()
+    for copy in scalars:
+        copy.wait()
     for slot in range(4):
         copies[2 * slot].wait()
         copies[2 * slot + 1].wait()
@@ -96,43 +101,10 @@
 
             lax.fori_loop(0, 2 * HALF // 8, body, 0, unroll=8)
 
-    for f in range(2):
-        for j in range(2):
-            block = jnp.transpose(acc[f, 128 * j : 128 * j + 128, :])
-            sums[f : f + 1, 128 * j : 128 * j + 128] = jnp.sum(block, axis=0, keepdims=True)
-
-
-def far_kernel(cols_hbm, count_hbm, c_hbm, e_hbm, out, cols, count, cbuf, ebuf, ssem, sem):
-    lon, core, lat = where_am_i()
-    scalars = fetch_scalars(cols_hbm, count_hbm, cols, count, ssem)
-    wanted = jnp.where(core == 1, 1, -2)
-    for copy in scalars:
-        copy.wait()
-
-    def need(slot):
-        return jnp.logical_and(slot < count[0], slot_place(cols, slot, lon)[1] == wanted)
-
-    def loads(slot):
-        return (
-            pltpu.make_async_copy(c_hbm.at[slot], cbuf.at[slot], sem.at[0, slot]),
-            pltpu.make_async_copy(e_hbm.at[slot], ebuf.at[slot], sem.at[1, slot]),
-        )
-
-    for slot in range(4):
-
-        @pl.when(need(slot))
-        def _(slot=slot):
-            for load in loads(slot):
-                load.start()
-
-    out[...] = jnp.zeros(out.shape, F32)
-    for slot in range(4):
-
-        @pl.when(need(slot))
-        def _(slot=slot):
-            for load in loads(slot):
-                load.wait()
-            within, _ = slot_place(cols, slot, lon)
+        within, rel = slot_place(cols, slot, lon)
+
+        @pl.when(jnp.logical_and(slot < count[0], rel == wanted))
+        def _(slot=slot, within=within):
             lane = iota((8, 128), 1)
 
             for first, start in ((0, HALF * (1 - lat)), (HALF, HALF * lat)):
@@ -149,6 +121,11 @@
                     return carry
 
                 lax.fori_loop(0, HALF // 8, body, 0, unroll=4)
+
+    for f in range(2):
+        for j in range(2):
+            block = jnp.transpose(acc[f, 128 * j : 128 * j + 128, :])
+            sums[f : f + 1, 128 * j : 128 * j + 128] = jnp.sum(block, axis=0, keepdims=True)
 
 
 def rolled(buf, slot, rows, within):
@@ -549,15 +526,16 @@
     inputs = (expo_col, expo_count, counts_blocks, exposure_blocks)
     scalars = [pltpu.SMEM((4,), jnp.int32), pltpu.SMEM((1,), jnp.int32)]
     semaphores = [pltpu.SemaphoreType.DMA((2,)), pltpu.SemaphoreType.DMA((2, 4))]
-    (sums,) = call(
-        sums_kernel,
-        [((2, 2 * HALF), F32)],
-        [ANY] * 3,
-        [pltpu.VMEM((2, 2 * HALF, 128), F32), scalars[1]]
+    b1, sums = call(
+        first_kernel,
+        [((2, 2 * HALF, TW), F32), ((2, 2 * HALF), F32)],
+        [ANY] * 4,
+        [pltpu.VMEM((2, 2 * HALF, 128), F32)]
+        + scalars
         + [pltpu.VMEM(blocks, jnp.int32), pltpu.VMEM(blocks, F32)]
-        + [pltpu.SemaphoreType.DMA(()), semaphores[1]],
+        + semaphores,
         limit=58,
-    )(*inputs[1:])
+    )(*inputs)
     sums = sums + on_lon(sums, partner)
     rest = call(
         rest_kernel,
@@ -573,13 +551,6 @@
     af = on_lon(af, partner)
     other = lax.ppermute(sums, "lat", [(0, 1), (1, 0)])
     sums = jnp.concatenate([sums, other], axis=0) + rest_token
-    (b1,) = call(
-        far_kernel,
-        [((2, 2 * HALF, TW), F32)],
-        [ANY] * 4,
-        scalars + [pltpu.VMEM(blocks, jnp.int32), pltpu.VMEM(blocks, F32)] + semaphores,
-        limit=58,
-    )(*inputs)
     b1 = on_lon(b1, two_out)
     steps = [sums]
     (b1_token,) = call(token_kernel, [(TOKEN, F32)], [ANY])(b1)

time: 71.5 us -> 70.1 us (0.980)
  Pallas kernels: 25.4 us -> 21.9 us
  starting transfers between devices: 28.8 us -> 30.4 us
    pallas_call x13 -> x12, Pallas kernels: 25.4 us -> 21.9 us  [run(): pl.pallas_call(body, out_shape=[jax.ShapeDtypeStruct(shape, dtype) for sh...]
    ppermute x14, starting transfers between devices: 23.4 us -> 25 us  [on_lon(): return lax.ppermute(value, 'lon', [(i, step(i) % LON) for i in range(LON)])]
  transfers between devices with their start and end apart: 16 -> 16, of which waited for: 9 -> 9; matrix products, arithmetic and copies ran while one was open for 1% -> 1% of each run, Pallas kernels for 22% -> 18%
where the time goes in v3:
time: 70.1 us; the launch traced here: 69.9 us
  starting transfers between devices  30.4 us (43%)
  Pallas kernels  21.9 us (31%)
  waiting for transfers between devices  15.9 us (23%)
  between operations  0.95 us (1%)
    ppermute x14, starting transfers between devices, on_lon(): return lax.ppermute(value, 'lon', [(i, step(i) % LON) for i in range(LON)])  25 us
    pallas_call x12, Pallas kernels, run(): pl.pallas_call(body, out_shape=[jax.ShapeDtypeStruct(shape, dtype) for sh...  21.9 us
    ppermute x14, waiting for transfers between devices, on_lon(): return lax.ppermute(value, 'lon', [(i, step(i) % LON) for i in range(LON)])  14.6 us
    ppermute x1, starting transfers between devices, per_device(): lat_rows = lax.ppermute(message, 'lat', [(0, 1), (1, 0)])  2.71 us
    ppermute x1, starting transfers between devices, per_device(): other = lax.ppermute(sums, 'lat', [(0, 1), (1, 0)])  2.62 us
  transfers between devices with their start and end apart: 16, of which 9 were waited for; matrix products, arithmetic and copies ran while one was open for 1% of the time, Pallas kernels for 18%

profile of v3, /device:TPU:1, one launch (start us, length us, event | category | flops | bytes accessed | tf_op | source)
XLA Modules:
  0.0 69.9 jit_solution(4235490723545971909)
XLA Ops:
  0.0 0.0 copy-start.2
  0.0 0.0 copy-start
  0.0 0.0 copy-start.1
  0.8 3.6 %shard_map.46 = (f32[2,256,512]{2,1,0:T(8,128)}, f32[2,256]{1,0:T(2,128)}) custom-call(s32[4]{0:T(128)} %refs_0_.3, s32[1]{0:T(128)S(6)} %copy.5.refs_1_, s32[4,256,512]{2,1,0:T(8,128)} %refs_2_.3, f32[4,256,512]{2,1,0:T(8,128)} %refs_3_.3), custom_call_target="tpu_custom_call" | custom-call | bytes 36000 | tf_op jit(solution)/shard_map/pallas_call | solution.py:473
  4.5 3.0 %collective-permute-start.2 = (f32[2,256,512]{2,1,0:T(8,128)}, f32[2,256,512]{2,1,0:T(8,128)S(1)}, u32[]{:S(2)}, u32[]{:S(2)}) collective-permute-start(f32[2,256,512]{2,1,0:T(8,128)} %get-tuple-element.42), channel_id=1, source_target_pairs={{0,252},{2,6},{4,0},{6,10},{8,4},{10,14},{12,8},{14,18},{16,12},{1... | collective-permute-start | bytes 3145736 | tf_op jit(solution)/shard_map/ppermute | solution.py:515
  7.5 9.7 %collective-permute-start = (f32[2,256]{1,0:T(2,128)}, f32[2,256]{1,0:T(2,128)S(1)}, u32[]{:S(2)}, u32[]{:S(2)}) collective-permute-start(f32[2,256]{1,0:T(2,128)} %get-tuple-element.38), channel_id=1, source_target_pairs={{0,2},{2,0},{4,6},{6,4},{8,10},{10,8},{12,14},{14,12},{16,18},{18,... | collective-permute-start | bytes 6152 | tf_op jit(solution)/shard_map/ppermute | solution.py:515
  17.2 1.0 %collective-permute-done = f32[2,256]{1,0:T(2,128)S(1)} collective-permute-done((f32[2,256]{1,0:T(2,128)}, f32[2,256]{1,0:T(2,128)S(1)}, u32[]{:S(2)}, u32[]{:S(2)}) %collective-permute-start) | collective-permute-done | bytes 2080 | tf_op jit(solution)/shard_map/ppermute | solution.py:515
  18.3 0.7 add.30.refs_4_
  18.9 0.0 copy-done.2
  18.9 0.0 copy-done
  18.9 0.0 copy-done.1
  18.9 2.9 %shard_map.47 = (f32[2,128,512]{2,1,0:T(8,128)S(1)}, f32[2,128,512]{2,1,0:T(8,128)S(1)}, f32[2,128,512]{2,1,0:T(8,128)S(1)}, f32[2,128,512]{2,1,0:T(8,128)S(1)},...) custom-call(s32[4]{0:T(128)S(1)} %copy-done.2, s32[1]{0:T(128)S(6)} %copy.5.refs_1_, ...), custom_call_target="tpu_custom_call" | custom-call | bytes 10800000 | tf_op jit(solution)/shard_map/pallas_call | solution.py:473
  21.9 0.4 collective-permute-start.1
  22.3 0.2 collective-permute-start.9
  22.5 2.6 %collective-permute-start.3 = (f32[2,256]{1,0:T(2,128)S(1)}, f32[2,256]{1,0:T(2,128)S(1)}, u32[]{:S(2)}, u32[]{:S(2)}) collective-permute-start(f32[2,256]{1,0:T(2,128)S(1)} %add.30.refs_4_), channel_id=1, source_target_pairs={{0,1},{1,0},{2,3},{3,2},{4,5},{5,4},{6,7},{7,6},{8,9},{9,8},{10,11... | collective-permute-start | bytes 6152 | tf_op jit(solution)/shard_map/ppermute | solution.py:552
  25.1 1.3 %collective-permute-done.3 = f32[2,256]{1,0:T(2,128)S(1)} collective-permute-done((f32[2,256]{1,0:T(2,128)S(1)}, f32[2,256]{1,0:T(2,128)S(1)}, u32[]{:S(2)}, u32[]{:S(2)}) %collective-permute-start.3) | collective-permute-done | bytes 2080 | tf_op jit(solution)/shard_map/ppermute | solution.py:552
  26.5 0.1 collective-permute-start.4
  26.6 0.0 collective-permute-done.2.refs_0_.refs_3_
  26.6 2.4 %collective-permute-done.4 = f32[4,256]{1,0:T(4,128)S(1)} collective-permute-done((f32[4,256]{1,0:T(4,128)S(1)}, f32[4,256]{1,0:T(4,128)S(1)}, u32[]{:S(2)}, u32[]{:S(2)}) %collective-permute-start.4) | collective-permute-done | bytes 4128 | tf_op jit(solution)/shard_map/ppermute | solution.py:515
  29.0 0.0 collective-permute-done.1.refs_2_
  29.0 0.2 shard_map.49
  29.2 0.1 collective-permute-start.5
  29.3 0.0 collective-permute-done.9.refs_2_
  29.3 0.2 shard_map.54
  29.6 1.8 %collective-permute-start.10 = (f32[2,136,512]{2,1,0:T(8,128)S(1)}, f32[2,136,512]{2,1,0:T(8,128)S(1)}, u32[]{:S(2)}, u32[]{:S(2)}) collective-permute-start(f32[2,136,512]{2,1,0:T(8,128)S(1)} %get-tuple-element.59.refs_2_), channel_id=1, source_target_pairs={{0,254},{2,4},{4,2},{6,8},{8,6},{10,12},{12,10},{14,16},{16,14},{1... | collective-permute-start | bytes 1671176 | tf_op jit(solution)/shard_map/ppermute | solution.py:515
  31.4 0.0 collective-permute-start.6
  31.4 2.5 %collective-permute-done.6 = f32[4,256]{1,0:T(4,128)S(1)} collective-permute-done((f32[4,256]{1,0:T(4,128)S(1)}, f32[4,256]{1,0:T(4,128)S(1)}, u32[]{:S(2)}, u32[]{:S(2)}) %collective-permute-start.6) | collective-permute-done | bytes 4128 | tf_op jit(solution)/shard_map/ppermute | solution.py:515
  33.8 0.0 collective-permute-start.7
  33.8 3.5 %shard_map.50 = (bf16[2,768,768]{2,1,0:T(8,128)(2,1)S(1)}, bf16[2,512,1152]{2,1,0:T(8,128)(2,1)S(1)}, bf16[3,128,960]{2,1,0:T(8,128)(2,1)S(1)}, bf16[3,128,1152]...) custom-call(f32[4,256]{1,0:T(4,128)S(1)} %add_add_fusion.1.refs_4_.r, ...), custom_call_target="tpu_custom_call" | custom-call | bytes 10800000 | tf_op jit(solution)/shard_map/pallas_call | solution.py:473
  37.4 0.4 collective-permute-done.7
  37.8 0.5 collective-permute-done.5.refs_1_
  38.3 0.2 shard_map.51
  38.5 8.9 %collective-permute-start.8 = (f32[2,8,512]{2,1,0:T(8,128)S(1)}, f32[2,8,512]{2,1,0:T(8,128)S(1)}, u32[]{:S(2)}, u32[]{:S(2)}) collective-permute-start(f32[2,8,512]{2,1,0:T(8,128)S(1)} %get-tuple-element.49), channel_id=1, source_target_pairs={{0,2},{2,0},{4,6},{6,4},{8,10},{10,8},{12,14},{14,12},{16,18},{18,... | collective-permute-start | bytes 98312 | tf_op jit(solution)/shard_map/ppermute | solution.py:515
  47.5 0.0 collective-permute-start.11
  47.5 0.9 %collective-permute-done.8.refs_2_ = f32[2,8,512]{2,1,0:T(8,128)S(1)} collective-permute-done((f32[2,8,512]{2,1,0:T(8,128)S(1)}, f32[2,8,512]{2,1,0:T(8,128)S(1)}, u32[]{:S(2)}, u32[]{:S(2)}) %collective-permute-start.8) | collective-permute-done | bytes 32800 | tf_op jit(solution)/shard_map/ppermute | solution.py:515
  48.3 0.2 shard_map.52
  48.5 2.7 %collective-permute-start.13 = (f32[2,32,768]{2,1,0:T(8,128)S(1)}, f32[2,32,768]{2,1,0:T(8,128)S(1)}, u32[]{:S(2)}, u32[]{:S(2)}) collective-permute-start(f32[2,32,768]{2,1,0:T(8,128)S(1)} %get-tuple-element.63), channel_id=1, source_target_pairs={{0,1},{1,0},{2,3},{3,2},{4,5},{5,4},{6,7},{7,6},{8,9},{9,8},{10,11... | collective-permute-start | bytes 589832 | tf_op jit(solution)/shard_map/ppermute | solution.py:594
  51.2 2.3 %shard_map.53 = (f32[3,4,128,512]{3,2,1,0:T(8,128)S(1)}, f32[3,3,128,512]{3,2,1,0:T(8,128)S(1)}, f32[4,256]{1,0:T(4,128)S(1)}) custom-call(f32[2,128,512]{2,1,0:T(8,128)S(1)} %get-tuple-element.47.refs_0_, f32[2,128,256]{2,1,0:T(8,128)S(1)} %get-tuple-element.50.refs_1_, bf16[2,768,768]{2,1,0:T(8,128)(2,1)S(1)} %get-tuple-element.51.refs_2_.refs_4_, ...), custom_call_target="tpu_custom_call" | custom-call | bytes 14400000 | tf_op jit(solution)/shard_map/pallas_call | solution.py:473
  53.5 0.0 collective-permute-done.11
  53.5 0.0 collective-permute-done.10.refs_1_
  53.5 0.2 shard_map.55
  53.8 0.7 %collective-permute-start.12 = (f32[2,8,512]{2,1,0:T(8,128)S(1)}, f32[2,8,512]{2,1,0:T(8,128)S(1)}, u32[]{:S(2)}, u32[]{:S(2)}) collective-permute-start(f32[2,8,512]{2,1,0:T(8,128)S(1)} %get-tuple-element.62), channel_id=1, source_target_pairs={{0,2},{2,0},{4,6},{6,4},{8,10},{10,8},{12,14},{14,12},{16,18},{18,... | collective-permute-start | bytes 98312 | tf_op jit(solution)/shard_map/ppermute | solution.py:515
  54.5 0.0 collective-permute-start.14
  54.5 3.4 %collective-permute-done.14 = f32[4,256]{1,0:T(4,128)S(1)} collective-permute-done((f32[4,256]{1,0:T(4,128)S(1)}, f32[4,256]{1,0:T(4,128)S(1)}, u32[]{:S(2)}, u32[]{:S(2)}) %collective-permute-start.14) | collective-permute-done | bytes 4128 | tf_op jit(solution)/shard_map/ppermute | solution.py:515
  57.9 0.0 collective-permute-start.15
  57.9 0.0 collective-permute-done.12.refs_2_
  57.9 0.0 collective-permute-done.13.refs_3_
  57.9 2.8 %shard_map.56 = (f32[3,4,160,512]{3,2,1,0:T(8,128)S(1)}, f32[3,3,160,512]{3,2,1,0:T(8,128)S(1)}) custom-call(f32[2,128,512]{2,1,0:T(8,128)S(1)} %get-tuple-element.60.refs_0_, f32[2,128,128]{2,1,0:T(8,128)S(1)} %get-tuple-element.61.refs_1_, f32[2,8,512]{2,1,0:T(8,128)S(1)} %collective-permute-done.12.refs_2_, ...), custom_call_target="tpu_custom_call" | custom-call | bytes 18000000 | tf_op jit(solution)/shard_map/pallas_call | solution.py:473
  60.7 3.5 %collective-permute-done.15.refs_5_ = f32[4,256]{1,0:T(4,128)S(1)} collective-permute-done((f32[4,256]{1,0:T(4,128)S(1)}, f32[4,256]{1,0:T(4,128)S(1)}, u32[]{:S(2)}, u32[]{:S(2)}) %collective-permute-start.15) | collective-permute-done | bytes 4128 | tf_op jit(solution)/shard_map/ppermute | solution.py:515
  64.3 5.6 %shard_map.57 = f32[3,256,512]{2,1,0:T(8,128)} custom-call(f32[3,4,128,512]{3,2,1,0:T(8,128)S(1)} %get-tuple-element.53.refs_0_, f32[3,3,128,512]{3,2,1,0:T(8,128)S(1)} %get-tuple-element.54.refs_1_, f32[3,4,160,512]{3,2,1,0:T(8,128)S(1)} %get-tuple-element.64.refs_2_, f32[3,3,160,512]{3,2,1,0:T(8,128)S(1)} %get-tuple-element.65.refs_3_, ...), custom_call_target="tpu_custom_call" | custom-call | bytes 36000 | tf_op jit(solution)/shard_map/pallas_call | solution.py:473
  (7 shorter events, 0.0 us)
Async XLA Ops:
  0.0 18.9 %copy-start.2 = (s32[4]{0:T(128)S(1)}, s32[4]{0:T(128)}, u32[]{:S(2)}) copy-start(s32[4]{0:T(128)} %refs_0_.3) | copy-start | bytes 52
  0.0 18.9 %copy-start = (s32[4,256,512]{2,1,0:T(8,128)S(1)}, s32[4,256,512]{2,1,0:T(8,128)}, u32[]{:S(2)}) copy-start(s32[4,256,512]{2,1,0:T(8,128)} %refs_2_.3) | copy-start | bytes 6291460
  0.0 18.9 %copy-start.1 = (f32[4,256,512]{2,1,0:T(8,128)S(1)}, f32[4,256,512]{2,1,0:T(8,128)}, u32[]{:S(2)}) copy-start(f32[4,256,512]{2,1,0:T(8,128)} %refs_3_.3) | copy-start | bytes 6291460
  4.5 22.1 %collective-permute-start.2 = (f32[2,256,512]{2,1,0:T(8,128)}, f32[2,256,512]{2,1,0:T(8,128)S(1)}, u32[]{:S(2)}, u32[]{:S(2)}) collective-permute-start(f32[2,256,512]{2,1,0:T(8,128)} %get-tuple-element.42), channel_id=1, source_target_pairs={{0,252},{2,6},{4,0},{6,10},{8,4},{10,14},{12,8},{14,18},{16,12},{1... | collective-permute-start | bytes 3145736 | tf_op jit(solution)/shard_map/ppermute | solution.py:515
  7.5 10.8 %collective-permute-start = (f32[2,256]{1,0:T(2,128)}, f32[2,256]{1,0:T(2,128)S(1)}, u32[]{:S(2)}, u32[]{:S(2)}) collective-permute-start(f32[2,256]{1,0:T(2,128)} %get-tuple-element.38), channel_id=1, source_target_pairs={{0,2},{2,0},{4,6},{6,4},{8,10},{10,8},{12,14},{14,12},{16,18},{18,... | collective-permute-start | bytes 6152 | tf_op jit(solution)/shard_map/ppermute | solution.py:515
  21.9 7.1 %collective-permute-start.1 = (f32[2,2,128,512]{3,2,1,0:T(8,128)S(1)}, f32[2,2,128,512]{3,2,1,0:T(8,128)S(1)}, u32[]{:S(2)}, u32[]{:S(2)}) collective-permute-start(f32[2,2,128,512]{3,2,1,0:T(8,128)S(1)} %get-tuple-element.41), channel_id=1, source_target_pairs={{0,2},{2,0},{4,6},{6,4},{8,10},{10,8},{12,14},{14,12},{16,18},{18,... | collective-permute-start | bytes 3145736 | tf_op jit(solution)/shard_map/ppermute | solution.py:515
  22.3 7.0 %collective-permute-start.9 = (f32[2,2,128,512]{3,2,1,0:T(8,128)S(1)}, f32[2,2,128,512]{3,2,1,0:T(8,128)S(1)}, u32[]{:S(2)}, u32[]{:S(2)}) collective-permute-start(f32[2,2,128,512]{3,2,1,0:T(8,128)S(1)} %get-tuple-element.57), channel_id=1, source_target_pairs={{0,2},{2,0},{4,6},{6,4},{8,10},{10,8},{12,14},{14,12},{16,18},{18,... | collective-permute-start | bytes 3145736 | tf_op jit(solution)/shard_map/ppermute | solution.py:515
  22.5 3.9 %collective-permute-start.3 = (f32[2,256]{1,0:T(2,128)S(1)}, f32[2,256]{1,0:T(2,128)S(1)}, u32[]{:S(2)}, u32[]{:S(2)}) collective-permute-start(f32[2,256]{1,0:T(2,128)S(1)} %add.30.refs_4_), channel_id=1, source_target_pairs={{0,1},{1,0},{2,3},{3,2},{4,5},{5,4},{6,7},{7,6},{8,9},{9,8},{10,11... | collective-permute-start | bytes 6152 | tf_op jit(solution)/shard_map/ppermute | solution.py:552
  26.5 2.5 %collective-permute-start.4 = (f32[4,256]{1,0:T(4,128)S(1)}, f32[4,256]{1,0:T(4,128)S(1)}, u32[]{:S(2)}, u32[]{:S(2)}) collective-permute-start(f32[4,256]{1,0:T(4,128)S(1)} %maximum_add_fusion), channel_id=1, source_target_pairs={{0,32},{2,34},{4,36},{6,38},{8,40},{10,42},{12,44},{14,46},{16,48}... | collective-permute-start | bytes 12296 | tf_op jit(solution)/shard_map/ppermute | solution.py:515
  29.2 9.0 %collective-permute-start.5 = (f32[2,136,512]{2,1,0:T(8,128)S(1)}, f32[2,136,512]{2,1,0:T(8,128)S(1)}, u32[]{:S(2)}, u32[]{:S(2)}) collective-permute-start(f32[2,136,512]{2,1,0:T(8,128)S(1)} %get-tuple-element.45.refs_2_), channel_id=1, source_target_pairs={{0,254},{2,4},{4,2},{6,8},{8,6},{10,12},{12,10},{14,16},{16,14},{1... | collective-permute-start | bytes 1671176 | tf_op jit(solution)/shard_map/ppermute | solution.py:515
  29.6 24.0 %collective-permute-start.10 = (f32[2,136,512]{2,1,0:T(8,128)S(1)}, f32[2,136,512]{2,1,0:T(8,128)S(1)}, u32[]{:S(2)}, u32[]{:S(2)}) collective-permute-start(f32[2,136,512]{2,1,0:T(8,128)S(1)} %get-tuple-element.59.refs_2_), channel_id=1, source_target_pairs={{0,254},{2,4},{4,2},{6,8},{8,6},{10,12},{12,10},{14,16},{16,14},{1... | collective-permute-start | bytes 1671176 | tf_op jit(solution)/shard_map/ppermute | solution.py:515
  31.4 2.5 %collective-permute-start.6 = (f32[4,256]{1,0:T(4,128)S(1)}, f32[4,256]{1,0:T(4,128)S(1)}, u32[]{:S(2)}, u32[]{:S(2)}) collective-permute-start(f32[4,256]{1,0:T(4,128)S(1)} %add_add_fusion.1.refs_4_.refs_0_), channel_id=1, source_target_pairs={{0,64},{2,66},{4,68},{6,70},{8,72},{10,74},{12,76},{14,78},{16,80}... | collective-permute-start | bytes 12296 | tf_op jit(solution)/shard_map/ppermute | solution.py:515
  33.8 4.0 %collective-permute-start.7 = (f32[4,256]{1,0:T(4,128)S(1)}, f32[4,256]{1,0:T(4,128)S(1)}, u32[]{:S(2)}, u32[]{:S(2)}) collective-permute-start(f32[4,256]{1,0:T(4,128)S(1)} %add.34), channel_id=1, source_target_pairs={{0,128},{2,130},{4,132},{6,134},{8,136},{10,138},{12,140},{14,142}... | collective-permute-start | bytes 12296 | tf_op jit(solution)/shard_map/ppermute | solution.py:515
  38.5 9.8 %collective-permute-start.8 = (f32[2,8,512]{2,1,0:T(8,128)S(1)}, f32[2,8,512]{2,1,0:T(8,128)S(1)}, u32[]{:S(2)}, u32[]{:S(2)}) collective-permute-start(f32[2,8,512]{2,1,0:T(8,128)S(1)} %get-tuple-element.49), channel_id=1, source_target_pairs={{0,2},{2,0},{4,6},{6,4},{8,10},{10,8},{12,14},{14,12},{16,18},{18,... | collective-permute-start | bytes 98312 | tf_op jit(solution)/shard_map/ppermute | solution.py:515
  47.5 6.0 %collective-permute-start.11 = (f32[4,256]{1,0:T(4,128)S(1)}, f32[4,256]{1,0:T(4,128)S(1)}, u32[]{:S(2)}, u32[]{:S(2)}) collective-permute-start(f32[4,256]{1,0:T(4,128)S(1)} %add_add_fusion.refs_3_), channel_id=1, source_target_pairs={{0,4},{2,6},{4,0},{6,2},{8,12},{10,14},{12,8},{14,10},{16,20},{18,... | collective-permute-start | bytes 12296 | tf_op jit(solution)/shard_map/ppermute | solution.py:515
  48.5 9.4 %collective-permute-start.13 = (f32[2,32,768]{2,1,0:T(8,128)S(1)}, f32[2,32,768]{2,1,0:T(8,128)S(1)}, u32[]{:S(2)}, u32[]{:S(2)}) collective-permute-start(f32[2,32,768]{2,1,0:T(8,128)S(1)} %get-tuple-element.63), channel_id=1, source_target_pairs={{0,1},{1,0},{2,3},{3,2},{4,5},{5,4},{6,7},{7,6},{8,9},{9,8},{10,11... | collective-permute-start | bytes 589832 | tf_op jit(solution)/shard_map/ppermute | solution.py:594
  53.8 4.1 %collective-permute-start.12 = (f32[2,8,512]{2,1,0:T(8,128)S(1)}, f32[2,8,512]{2,1,0:T(8,128)S(1)}, u32[]{:S(2)}, u32[]{:S(2)}) collective-permute-start(f32[2,8,512]{2,1,0:T(8,128)S(1)} %get-tuple-element.62), channel_id=1, source_target_pairs={{0,2},{2,0},{4,6},{6,4},{8,10},{10,8},{12,14},{14,12},{16,18},{18,... | collective-permute-start | bytes 98312 | tf_op jit(solution)/shard_map/ppermute | solution.py:515
  54.5 3.4 %collective-permute-start.14 = (f32[4,256]{1,0:T(4,128)S(1)}, f32[4,256]{1,0:T(4,128)S(1)}, u32[]{:S(2)}, u32[]{:S(2)}) collective-permute-start(f32[4,256]{1,0:T(4,128)S(1)} %get-tuple-element.71), channel_id=1, source_target_pairs={{0,8},{2,10},{4,12},{6,14},{8,0},{10,2},{12,4},{14,6},{16,24},{18,... | collective-permute-start | bytes 12296 | tf_op jit(solution)/shard_map/ppermute | solution.py:515
  57.9 6.4 %collective-permute-start.15 = (f32[4,256]{1,0:T(4,128)S(1)}, f32[4,256]{1,0:T(4,128)S(1)}, u32[]{:S(2)}, u32[]{:S(2)}) collective-permute-start(f32[4,256]{1,0:T(4,128)S(1)} %add.39.refs_4_), channel_id=1, source_target_pairs={{0,16},{2,18},{4,20},{6,22},{8,24},{10,26},{12,28},{14,30},{16,0},... | collective-permute-start | bytes 12296 | tf_op jit(solution)/shard_map/ppermute | solution.py:515

commit v4 on v3

--- a/solution.py
+++ b/solution.py
@@ -543,7 +543,7 @@
         [ANY, ANY, VMEM, VMEM],
         [pltpu.VMEM((16, 8, TW), F32)] + scalars + semaphores[:1],
         after=[sums],
-        us=3.0,
+        us=1.0,
         limit=24,
     )
     q1n, q1f, q0n, q0f, an, af, rest_token = rest(*inputs)
@@ -586,7 +586,7 @@
     b2_n = on_lon(sent_n, one_out)
     partial_f, sent_f = merge(HALF, [steps[1]], q1f, q0f, af, b1)
     b2_f = on_lon(sent_f, one_out)
-    total_n, outer_n, inner_n = totals([steps[3]], partial_n, b2_n, sent_n)
+    total_n, outer_n, inner_n = totals([steps[2]], partial_n, b2_n, sent_n)
     inner_n = on_lon(inner_n, partner)
     wrap_n, message = call(
         seam_kernel, [((2, HALF, 256), F32), ((2, RAD, TW + 256), F32)], [VMEM] * 3

time: 70.1 us -> 67.7 us (0.966)
  the two profiles are of different devices: /device:TPU:1 before, /device:TPU:4 now
where the time goes in v4:
time: 67.7 us; the launch traced here: 67.6 us
  starting transfers between devices  23.6 us (35%)
  Pallas kernels  23 us (34%)
  waiting for transfers between devices  19.3 us (29%)
  between operations  0.99 us (1%)
  other arithmetic  0.7 us (1%)
    pallas_call x12, Pallas kernels, run(): pl.pallas_call(body, out_shape=[jax.ShapeDtypeStruct(shape, dtype) for sh...  23 us
    ppermute x14, starting transfers between devices, on_lon(): return lax.ppermute(value, 'lon', [(i, step(i) % LON) for i in range(LON)])  17.8 us
    ppermute x14, waiting for transfers between devices, on_lon(): return lax.ppermute(value, 'lon', [(i, step(i) % LON) for i in range(LON)])  16.9 us
    ppermute x1, starting transfers between devices, per_device(): other = lax.ppermute(sums, 'lat', [(0, 1), (1, 0)])  2.9 us
    ppermute x1, starting transfers between devices, per_device(): lat_rows = lax.ppermute(message, 'lat', [(0, 1), (1, 0)])  2.84 us
    ppermute x1, waiting for transfers between devices, per_device(): other = lax.ppermute(sums, 'lat', [(0, 1), (1, 0)])  2.34 us
  transfers between devices with their start and end apart: 16, of which 8 were waited for; matrix products, arithmetic and copies ran while one was open for 1% of the time, Pallas kernels for 19%

profile of v4, /device:TPU:4, one launch (start us, length us, event | category | flops | bytes accessed | tf_op | source)
XLA Modules:
  0.0 67.6 jit_solution(3316518399406451357)
XLA Ops:
  0.0 0.0 copy-start.2
  0.0 0.0 copy-start
  0.0 0.0 copy-start.1
  0.8 4.7 %shard_map.46 = (f32[2,256,512]{2,1,0:T(8,128)}, f32[2,256]{1,0:T(2,128)}) custom-call(s32[4]{0:T(128)} %refs_0_.3, s32[1]{0:T(128)S(6)} %copy.5.refs_1_, s32[4,256,512]{2,1,0:T(8,128)} %refs_2_.3, f32[4,256,512]{2,1,0:T(8,128)} %refs_3_.3), custom_call_target="tpu_custom_call" | custom-call | bytes 36000 | tf_op jit(solution)/shard_map/pallas_call | solution.py:473
  5.5 6.1 %collective-permute-start.2 = (f32[2,256,512]{2,1,0:T(8,128)}, f32[2,256,512]{2,1,0:T(8,128)S(1)}, u32[]{:S(2)}, u32[]{:S(2)}) collective-permute-start(f32[2,256,512]{2,1,0:T(8,128)} %get-tuple-element.42), channel_id=1, source_target_pairs={{0,252},{2,6},{4,0},{6,10},{8,4},{10,14},{12,8},{14,18},{16,12},{1... | collective-permute-start | bytes 3145736 | tf_op jit(solution)/shard_map/ppermute | solution.py:515
  11.7 0.0 collective-permute-start
  11.7 1.4 %collective-permute-done = f32[2,256]{1,0:T(2,128)S(1)} collective-permute-done((f32[2,256]{1,0:T(2,128)}, f32[2,256]{1,0:T(2,128)S(1)}, u32[]{:S(2)}, u32[]{:S(2)}) %collective-permute-start) | collective-permute-done | bytes 2080 | tf_op jit(solution)/shard_map/ppermute | solution.py:515
  13.0 0.7 add.30.refs_4_
  13.7 0.0 copy-done.2
  13.7 0.0 copy-done
  13.7 0.0 copy-done.1
  13.7 2.9 %shard_map.47 = (f32[2,128,512]{2,1,0:T(8,128)S(1)}, f32[2,128,512]{2,1,0:T(8,128)S(1)}, f32[2,128,512]{2,1,0:T(8,128)S(1)}, f32[2,128,512]{2,1,0:T(8,128)S(1)},...) custom-call(s32[4]{0:T(128)S(1)} %copy-done.2, s32[1]{0:T(128)S(6)} %copy.5.refs_1_, ...), custom_call_target="tpu_custom_call" | custom-call | bytes 3600000 | tf_op jit(solution)/shard_map/pallas_call | solution.py:473
  16.6 0.3 collective-permute-start.1
  16.9 0.3 collective-permute-start.8
  17.2 2.9 %collective-permute-start.3 = (f32[2,256]{1,0:T(2,128)S(1)}, f32[2,256]{1,0:T(2,128)S(1)}, u32[]{:S(2)}, u32[]{:S(2)}) collective-permute-start(f32[2,256]{1,0:T(2,128)S(1)} %add.30.refs_4_), channel_id=1, source_target_pairs={{0,1},{1,0},{2,3},{3,2},{4,5},{5,4},{6,7},{7,6},{8,9},{9,8},{10,11... | collective-permute-start | bytes 6152 | tf_op jit(solution)/shard_map/ppermute | solution.py:552
  20.1 2.3 %collective-permute-done.3 = f32[2,256]{1,0:T(2,128)S(1)} collective-permute-done((f32[2,256]{1,0:T(2,128)S(1)}, f32[2,256]{1,0:T(2,128)S(1)}, u32[]{:S(2)}, u32[]{:S(2)}) %collective-permute-start.3) | collective-permute-done | bytes 2080 | tf_op jit(solution)/shard_map/ppermute | solution.py:552
  22.5 0.3 collective-permute-start.4
  22.8 1.5 %collective-permute-done.2.refs_0_.refs_3_ = f32[2,256,512]{2,1,0:T(8,128)S(1)} collective-permute-done((f32[2,256,512]{2,1,0:T(8,128)}, f32[2,256,512]{2,1,0:T(8,128)S(1)}, u32[]{:S(2)}, u32[]{:S(2)}) %collective-permute-start.2) | collective-permute-done | bytes 1048608 | tf_op jit(solution)/shard_map/ppermute | solution.py:515
  24.3 1.9 %collective-permute-done.4 = f32[4,256]{1,0:T(4,128)S(1)} collective-permute-done((f32[4,256]{1,0:T(4,128)S(1)}, f32[4,256]{1,0:T(4,128)S(1)}, u32[]{:S(2)}, u32[]{:S(2)}) %collective-permute-start.4) | collective-permute-done | bytes 4128 | tf_op jit(solution)/shard_map/ppermute | solution.py:515
  26.2 0.0 collective-permute-done.1.refs_2_
  26.2 0.2 shard_map.49
  26.4 0.1 collective-permute-start.5
  26.5 0.0 collective-permute-done.8.refs_2_
  26.5 0.2 shard_map.54
  26.7 4.8 %collective-permute-start.9 = (f32[2,136,512]{2,1,0:T(8,128)S(1)}, f32[2,136,512]{2,1,0:T(8,128)S(1)}, u32[]{:S(2)}, u32[]{:S(2)}) collective-permute-start(f32[2,136,512]{2,1,0:T(8,128)S(1)} %get-tuple-element.58.refs_2_), channel_id=1, source_target_pairs={{0,254},{2,4},{4,2},{6,8},{8,6},{10,12},{12,10},{14,16},{16,14},{1... | collective-permute-start | bytes 1671176 | tf_op jit(solution)/shard_map/ppermute | solution.py:515
  31.6 1.7 %collective-permute-start.6 = (f32[4,256]{1,0:T(4,128)S(1)}, f32[4,256]{1,0:T(4,128)S(1)}, u32[]{:S(2)}, u32[]{:S(2)}) collective-permute-start(f32[4,256]{1,0:T(4,128)S(1)} %add_add_fusion.1.refs_4_.refs_0_), channel_id=1, source_target_pairs={{0,64},{2,66},{4,68},{6,70},{8,72},{10,74},{12,76},{14,78},{16,80}... | collective-permute-start | bytes 12296 | tf_op jit(solution)/shard_map/ppermute | solution.py:515
  33.3 1.9 %collective-permute-done.6 = f32[4,256]{1,0:T(4,128)S(1)} collective-permute-done((f32[4,256]{1,0:T(4,128)S(1)}, f32[4,256]{1,0:T(4,128)S(1)}, u32[]{:S(2)}, u32[]{:S(2)}) %collective-permute-start.6) | collective-permute-done | bytes 4128 | tf_op jit(solution)/shard_map/ppermute | solution.py:515
  35.2 3.7 %collective-permute-start.10 = (f32[4,256]{1,0:T(4,128)S(1)}, f32[4,256]{1,0:T(4,128)S(1)}, u32[]{:S(2)}, u32[]{:S(2)}) collective-permute-start(f32[4,256]{1,0:T(4,128)S(1)} %add.34.refs_3_), channel_id=1, source_target_pairs={{0,128},{2,130},{4,132},{6,134},{8,136},{10,138},{12,140},{14,142}... | collective-permute-start | bytes 12296 | tf_op jit(solution)/shard_map/ppermute | solution.py:515
  38.8 3.5 %shard_map.52 = (bf16[2,768,768]{2,1,0:T(8,128)(2,1)S(1)}, bf16[2,512,1152]{2,1,0:T(8,128)(2,1)S(1)}, bf16[3,128,960]{2,1,0:T(8,128)(2,1)S(1)}, bf16[3,128,1152]...) custom-call(f32[4,256]{1,0:T(4,128)S(1)} %add_add_fusion.1.refs_4_.r, ...), custom_call_target="tpu_custom_call" | custom-call | bytes 10800000 | tf_op jit(solution)/shard_map/pallas_call | solution.py:473
  42.4 0.0 collective-permute-done.5.refs_1_
  42.4 0.2 shard_map.50
  42.6 0.3 collective-permute-start.7
  42.9 0.0 collective-permute-done.10
  42.9 0.1 collective-permute-start.11
  43.0 1.1 %collective-permute-done.7.refs_2_ = f32[2,8,512]{2,1,0:T(8,128)S(1)} collective-permute-done((f32[2,8,512]{2,1,0:T(8,128)S(1)}, f32[2,8,512]{2,1,0:T(8,128)S(1)}, u32[]{:S(2)}, u32[]{:S(2)}) %collective-permute-start.7) | collective-permute-done | bytes 32800 | tf_op jit(solution)/shard_map/ppermute | solution.py:515
  44.1 0.2 shard_map.51
  44.3 2.8 %collective-permute-start.13 = (f32[2,32,768]{2,1,0:T(8,128)S(1)}, f32[2,32,768]{2,1,0:T(8,128)S(1)}, u32[]{:S(2)}, u32[]{:S(2)}) collective-permute-start(f32[2,32,768]{2,1,0:T(8,128)S(1)} %get-tuple-element.63), channel_id=1, source_target_pairs={{0,1},{1,0},{2,3},{3,2},{4,5},{5,4},{6,7},{7,6},{8,9},{9,8},{10,11... | collective-permute-start | bytes 589832 | tf_op jit(solution)/shard_map/ppermute | solution.py:594
  47.2 2.3 %shard_map.53 = (f32[3,4,128,512]{3,2,1,0:T(8,128)S(1)}, f32[3,3,128,512]{3,2,1,0:T(8,128)S(1)}, f32[4,256]{1,0:T(4,128)S(1)}) custom-call(f32[2,128,512]{2,1,0:T(8,128)S(1)} %get-tuple-element.46.refs_0_, f32[2,128,256]{2,1,0:T(8,128)S(1)} %get-tuple-element.49.refs_1_, bf16[2,768,768]{2,1,0:T(8,128)(2,1)S(1)} %get-tuple-element.50.refs_2_.refs_4_, ...), custom_call_target="tpu_custom_call" | custom-call | bytes 14400000 | tf_op jit(solution)/shard_map/pallas_call | solution.py:473
  49.4 0.0 collective-permute-done.11
  49.4 0.0 collective-permute-done.9.refs_1_
  49.5 0.2 shard_map.55
  49.7 0.1 collective-permute-start.12
  49.8 0.1 collective-permute-start.14
  49.9 4.5 %collective-permute-done.14 = f32[4,256]{1,0:T(4,128)S(1)} collective-permute-done((f32[4,256]{1,0:T(4,128)S(1)}, f32[4,256]{1,0:T(4,128)S(1)}, u32[]{:S(2)}, u32[]{:S(2)}) %collective-permute-start.14) | collective-permute-done | bytes 4128 | tf_op jit(solution)/shard_map/ppermute | solution.py:515
  54.4 0.0 collective-permute-start.15
  54.4 0.0 collective-permute-done.12.refs_2_
  54.4 0.0 collective-permute-done.13.refs_3_
  54.4 2.8 %shard_map.56 = (f32[3,4,160,512]{3,2,1,0:T(8,128)S(1)}, f32[3,3,160,512]{3,2,1,0:T(8,128)S(1)}) custom-call(f32[2,128,512]{2,1,0:T(8,128)S(1)} %get-tuple-element.60.refs_0_, f32[2,128,128]{2,1,0:T(8,128)S(1)} %get-tuple-element.61.refs_1_, f32[2,8,512]{2,1,0:T(8,128)S(1)} %collective-permute-done.12.refs_2_, ...), custom_call_target="tpu_custom_call" | custom-call | bytes 18000000 | tf_op jit(solution)/shard_map/pallas_call | solution.py:473
  57.2 4.7 %collective-permute-done.15.refs_5_ = f32[4,256]{1,0:T(4,128)S(1)} collective-permute-done((f32[4,256]{1,0:T(4,128)S(1)}, f32[4,256]{1,0:T(4,128)S(1)}, u32[]{:S(2)}, u32[]{:S(2)}) %collective-permute-start.15) | collective-permute-done | bytes 4128 | tf_op jit(solution)/shard_map/ppermute | solution.py:515
  61.9 5.6 %shard_map.57 = f32[3,256,512]{2,1,0:T(8,128)} custom-call(f32[3,4,128,512]{3,2,1,0:T(8,128)S(1)} %get-tuple-element.52.refs_0_, f32[3,3,128,512]{3,2,1,0:T(8,128)S(1)} %get-tuple-element.53.refs_1_, f32[3,4,160,512]{3,2,1,0:T(8,128)S(1)} %get-tuple-element.64.refs_2_, f32[3,3,160,512]{3,2,1,0:T(8,128)S(1)} %get-tuple-element.65.refs_3_, ...), custom_call_target="tpu_custom_call" | custom-call | bytes 36000 | tf_op jit(solution)/shard_map/pallas_call | solution.py:473
  (7 shorter events, 0.0 us)
Async XLA Ops:
  0.0 13.7 %copy-start.2 = (s32[4]{0:T(128)S(1)}, s32[4]{0:T(128)}, u32[]{:S(2)}) copy-start(s32[4]{0:T(128)} %refs_0_.3) | copy-start | bytes 52
  0.0 13.7 %copy-start = (s32[4,256,512]{2,1,0:T(8,128)S(1)}, s32[4,256,512]{2,1,0:T(8,128)}, u32[]{:S(2)}) copy-start(s32[4,256,512]{2,1,0:T(8,128)} %refs_2_.3) | copy-start | bytes 6291460
  0.0 13.7 %copy-start.1 = (f32[4,256,512]{2,1,0:T(8,128)S(1)}, f32[4,256,512]{2,1,0:T(8,128)}, u32[]{:S(2)}) copy-start(f32[4,256,512]{2,1,0:T(8,128)} %refs_3_.3) | copy-start | bytes 6291460
  5.5 18.7 %collective-permute-start.2 = (f32[2,256,512]{2,1,0:T(8,128)}, f32[2,256,512]{2,1,0:T(8,128)S(1)}, u32[]{:S(2)}, u32[]{:S(2)}) collective-permute-start(f32[2,256,512]{2,1,0:T(8,128)} %get-tuple-element.42), channel_id=1, source_target_pairs={{0,252},{2,6},{4,0},{6,10},{8,4},{10,14},{12,8},{14,18},{16,12},{1... | collective-permute-start | bytes 3145736 | tf_op jit(solution)/shard_map/ppermute | solution.py:515
  11.7 1.4 %collective-permute-start = (f32[2,256]{1,0:T(2,128)}, f32[2,256]{1,0:T(2,128)S(1)}, u32[]{:S(2)}, u32[]{:S(2)}) collective-permute-start(f32[2,256]{1,0:T(2,128)} %get-tuple-element.38), channel_id=1, source_target_pairs={{0,2},{2,0},{4,6},{6,4},{8,10},{10,8},{12,14},{14,12},{16,18},{18,... | collective-permute-start | bytes 6152 | tf_op jit(solution)/shard_map/ppermute | solution.py:515
  16.6 9.5 %collective-permute-start.1 = (f32[2,2,128,512]{3,2,1,0:T(8,128)S(1)}, f32[2,2,128,512]{3,2,1,0:T(8,128)S(1)}, u32[]{:S(2)}, u32[]{:S(2)}) collective-permute-start(f32[2,2,128,512]{3,2,1,0:T(8,128)S(1)} %get-tuple-element.41), channel_id=1, source_target_pairs={{0,2},{2,0},{4,6},{6,4},{8,10},{10,8},{12,14},{14,12},{16,18},{18,... | collective-permute-start | bytes 3145736 | tf_op jit(solution)/shard_map/ppermute | solution.py:515
  16.9 9.6 %collective-permute-start.8 = (f32[2,2,128,512]{3,2,1,0:T(8,128)S(1)}, f32[2,2,128,512]{3,2,1,0:T(8,128)S(1)}, u32[]{:S(2)}, u32[]{:S(2)}) collective-permute-start(f32[2,2,128,512]{3,2,1,0:T(8,128)S(1)} %get-tuple-element.56), channel_id=1, source_target_pairs={{0,2},{2,0},{4,6},{6,4},{8,10},{10,8},{12,14},{14,12},{16,18},{18,... | collective-permute-start | bytes 3145736 | tf_op jit(solution)/shard_map/ppermute | solution.py:515
  17.2 5.2 %collective-permute-start.3 = (f32[2,256]{1,0:T(2,128)S(1)}, f32[2,256]{1,0:T(2,128)S(1)}, u32[]{:S(2)}, u32[]{:S(2)}) collective-permute-start(f32[2,256]{1,0:T(2,128)S(1)} %add.30.refs_4_), channel_id=1, source_target_pairs={{0,1},{1,0},{2,3},{3,2},{4,5},{5,4},{6,7},{7,6},{8,9},{9,8},{10,11... | collective-permute-start | bytes 6152 | tf_op jit(solution)/shard_map/ppermute | solution.py:552
  22.5 3.7 %collective-permute-start.4 = (f32[4,256]{1,0:T(4,128)S(1)}, f32[4,256]{1,0:T(4,128)S(1)}, u32[]{:S(2)}, u32[]{:S(2)}) collective-permute-start(f32[4,256]{1,0:T(4,128)S(1)} %maximum_add_fusion), channel_id=1, source_target_pairs={{0,32},{2,34},{4,36},{6,38},{8,40},{10,42},{12,44},{14,46},{16,48}... | collective-permute-start | bytes 12296 | tf_op jit(solution)/shard_map/ppermute | solution.py:515
  26.4 16.0 %collective-permute-start.5 = (f32[2,136,512]{2,1,0:T(8,128)S(1)}, f32[2,136,512]{2,1,0:T(8,128)S(1)}, u32[]{:S(2)}, u32[]{:S(2)}) collective-permute-start(f32[2,136,512]{2,1,0:T(8,128)S(1)} %get-tuple-element.45.refs_2_), channel_id=1, source_target_pairs={{0,254},{2,4},{4,2},{6,8},{8,6},{10,12},{12,10},{14,16},{16,14},{1... | collective-permute-start | bytes 1671176 | tf_op jit(solution)/shard_map/ppermute | solution.py:515
  26.7 22.7 %collective-permute-start.9 = (f32[2,136,512]{2,1,0:T(8,128)S(1)}, f32[2,136,512]{2,1,0:T(8,128)S(1)}, u32[]{:S(2)}, u32[]{:S(2)}) collective-permute-start(f32[2,136,512]{2,1,0:T(8,128)S(1)} %get-tuple-element.58.refs_2_), channel_id=1, source_target_pairs={{0,254},{2,4},{4,2},{6,8},{8,6},{10,12},{12,10},{14,16},{16,14},{1... | collective-permute-start | bytes 1671176 | tf_op jit(solution)/shard_map/ppermute | solution.py:515
  31.6 3.6 %collective-permute-start.6 = (f32[4,256]{1,0:T(4,128)S(1)}, f32[4,256]{1,0:T(4,128)S(1)}, u32[]{:S(2)}, u32[]{:S(2)}) collective-permute-start(f32[4,256]{1,0:T(4,128)S(1)} %add_add_fusion.1.refs_4_.refs_0_), channel_id=1, source_target_pairs={{0,64},{2,66},{4,68},{6,70},{8,72},{10,74},{12,76},{14,78},{16,80}... | collective-permute-start | bytes 12296 | tf_op jit(solution)/shard_map/ppermute | solution.py:515
  35.2 7.7 %collective-permute-start.10 = (f32[4,256]{1,0:T(4,128)S(1)}, f32[4,256]{1,0:T(4,128)S(1)}, u32[]{:S(2)}, u32[]{:S(2)}) collective-permute-start(f32[4,256]{1,0:T(4,128)S(1)} %add.34.refs_3_), channel_id=1, source_target_pairs={{0,128},{2,130},{4,132},{6,134},{8,136},{10,138},{12,140},{14,142}... | collective-permute-start | bytes 12296 | tf_op jit(solution)/shard_map/ppermute | solution.py:515
  42.6 1.5 %collective-permute-start.7 = (f32[2,8,512]{2,1,0:T(8,128)S(1)}, f32[2,8,512]{2,1,0:T(8,128)S(1)}, u32[]{:S(2)}, u32[]{:S(2)}) collective-permute-start(f32[2,8,512]{2,1,0:T(8,128)S(1)} %get-tuple-element.48), channel_id=1, source_target_pairs={{0,2},{2,0},{4,6},{6,4},{8,10},{10,8},{12,14},{14,12},{16,18},{18,... | collective-permute-start | bytes 98312 | tf_op jit(solution)/shard_map/ppermute | solution.py:515
  42.9 6.5 %collective-permute-start.11 = (f32[4,256]{1,0:T(4,128)S(1)}, f32[4,256]{1,0:T(4,128)S(1)}, u32[]{:S(2)}, u32[]{:S(2)}) collective-permute-start(f32[4,256]{1,0:T(4,128)S(1)} %add_add_fusion), channel_id=1, source_target_pairs={{0,4},{2,6},{4,0},{6,2},{8,12},{10,14},{12,8},{14,10},{16,20},{18,... | collective-permute-start | bytes 12296 | tf_op jit(solution)/shard_map/ppermute | solution.py:515
  44.3 10.1 %collective-permute-start.13 = (f32[2,32,768]{2,1,0:T(8,128)S(1)}, f32[2,32,768]{2,1,0:T(8,128)S(1)}, u32[]{:S(2)}, u32[]{:S(2)}) collective-permute-start(f32[2,32,768]{2,1,0:T(8,128)S(1)} %get-tuple-element.63), channel_id=1, source_target_pairs={{0,1},{1,0},{2,3},{3,2},{4,5},{5,4},{6,7},{7,6},{8,9},{9,8},{10,11... | collective-permute-start | bytes 589832 | tf_op jit(solution)/shard_map/ppermute | solution.py:594
  49.7 4.7 %collective-permute-start.12 = (f32[2,8,512]{2,1,0:T(8,128)S(1)}, f32[2,8,512]{2,1,0:T(8,128)S(1)}, u32[]{:S(2)}, u32[]{:S(2)}) collective-permute-start(f32[2,8,512]{2,1,0:T(8,128)S(1)} %get-tuple-element.62), channel_id=1, source_target_pairs={{0,2},{2,0},{4,6},{6,4},{8,10},{10,8},{12,14},{14,12},{16,18},{18,... | collective-permute-start | bytes 98312 | tf_op jit(solution)/shard_map/ppermute | solution.py:515
  49.8 4.6 %collective-permute-start.14 = (f32[4,256]{1,0:T(4,128)S(1)}, f32[4,256]{1,0:T(4,128)S(1)}, u32[]{:S(2)}, u32[]{:S(2)}) collective-permute-start(f32[4,256]{1,0:T(4,128)S(1)} %get-tuple-element.71), channel_id=1, source_target_pairs={{0,8},{2,10},{4,12},{6,14},{8,0},{10,2},{12,4},{14,6},{16,24},{18,... | collective-permute-start | bytes 12296 | tf_op jit(solution)/shard_map/ppermute | solution.py:515
  54.4 7.5 %collective-permute-start.15 = (f32[4,256]{1,0:T(4,128)S(1)}, f32[4,256]{1,0:T(4,128)S(1)}, u32[]{:S(2)}, u32[]{:S(2)}) collective-permute-start(f32[4,256]{1,0:T(4,128)S(1)} %add.39.refs_4_), channel_id=1, source_target_pairs={{0,16},{2,18},{4,20},{6,22},{8,24},{10,26},{12,28},{14,30},{16,0},... | collective-permute-start | bytes 12296 | tf_op jit(solution)/shard_map/ppermute | solution.py:515

commit v5 on v4

--- a/solution.py
+++ b/solution.py
@@ -602,7 +602,7 @@
     sums = sums + near_token
     sums = sums + on_lon(sums, lambda i: i ^ 4)
     last = on_lon(sums, lambda i: i ^ 8)
-    total_f, outer_f, inner_f = totals([steps[4]], partial_f, b2_f, sent_f)
+    total_f, outer_f, inner_f = totals([steps[3]], partial_f, b2_f, sent_f)
     inner_f = on_lon(inner_f, partner)
     far_wave, far_vari = call(
         far_columns_kernel,

time: 67.7 us -> 70.6 us (1.043)
  the two profiles are of different devices: /device:TPU:4 before, /device:TPU:1 now
where the time goes in v5:
time: 70.6 us; the launch traced here: 70.7 us
  starting transfers between devices  31.3 us (44%)
  Pallas kernels  23.1 us (33%)
  waiting for transfers between devices  14.7 us (21%)
  between operations  0.96 us (1%)
  other arithmetic  0.71 us (1%)
    ppermute x14, starting transfers between devices, on_lon(): return lax.ppermute(value, 'lon', [(i, step(i) % LON) for i in range(LON)])  26.1 us
    pallas_call x12, Pallas kernels, run(): pl.pallas_call(body, out_shape=[jax.ShapeDtypeStruct(shape, dtype) for sh...  23.1 us
    ppermute x14, waiting for transfers between devices, on_lon(): return lax.ppermute(value, 'lon', [(i, step(i) % LON) for i in range(LON)])  13.1 us
    ppermute x1, starting transfers between devices, per_device(): other = lax.ppermute(sums, 'lat', [(0, 1), (1, 0)])  2.62 us
    ppermute x1, starting transfers between devices, per_device(): lat_rows = lax.ppermute(message, 'lat', [(0, 1), (1, 0)])  2.56 us
    ppermute x1, waiting for transfers between devices, per_device(): other = lax.ppermute(sums, 'lat', [(0, 1), (1, 0)])  1.53 us
  transfers between devices with their start and end apart: 16, of which 6 were waited for; matrix products, arithmetic and copies ran while one was open for 1% of the time, Pallas kernels for 18%

profile of v5, /device:TPU:1, one launch (start us, length us, event | category | flops | bytes accessed | tf_op | source)
XLA Modules:
  0.0 70.7 jit_solution(7970864590900220947)
XLA Ops:
  0.0 0.0 copy-start.2
  0.0 0.0 copy-start.1
  0.0 0.0 copy-start
  0.8 4.8 %shard_map.46 = (f32[2,256,512]{2,1,0:T(8,128)}, f32[2,256]{1,0:T(2,128)}) custom-call(s32[4]{0:T(128)} %refs_0_.3, s32[1]{0:T(128)S(6)} %copy.5.refs_1_, s32[4,256,512]{2,1,0:T(8,128)} %refs_2_.3, f32[4,256,512]{2,1,0:T(8,128)} %refs_3_.3), custom_call_target="tpu_custom_call" | custom-call | bytes 36000 | tf_op jit(solution)/shard_map/pallas_call | solution.py:473
  5.6 1.5 %collective-permute-start.2 = (f32[2,256,512]{2,1,0:T(8,128)}, f32[2,256,512]{2,1,0:T(8,128)S(1)}, u32[]{:S(2)}, u32[]{:S(2)}) collective-permute-start(f32[2,256,512]{2,1,0:T(8,128)} %get-tuple-element.42), channel_id=1, source_target_pairs={{0,252},{2,6},{4,0},{6,10},{8,4},{10,14},{12,8},{14,18},{16,12},{1... | collective-permute-start | bytes 3145736 | tf_op jit(solution)/shard_map/ppermute | solution.py:515
  7.1 8.5 %collective-permute-start = (f32[2,256]{1,0:T(2,128)}, f32[2,256]{1,0:T(2,128)S(1)}, u32[]{:S(2)}, u32[]{:S(2)}) collective-permute-start(f32[2,256]{1,0:T(2,128)} %get-tuple-element.38), channel_id=1, source_target_pairs={{0,2},{2,0},{4,6},{6,4},{8,10},{10,8},{12,14},{14,12},{16,18},{18,... | collective-permute-start | bytes 6152 | tf_op jit(solution)/shard_map/ppermute | solution.py:515
  15.6 1.0 %collective-permute-done = f32[2,256]{1,0:T(2,128)S(1)} collective-permute-done((f32[2,256]{1,0:T(2,128)}, f32[2,256]{1,0:T(2,128)S(1)}, u32[]{:S(2)}, u32[]{:S(2)}) %collective-permute-start) | collective-permute-done | bytes 2080 | tf_op jit(solution)/shard_map/ppermute | solution.py:515
  16.6 0.7 add.30.refs_4_
  17.3 0.0 copy-done.2
  17.3 0.0 copy-done.1
  17.3 0.0 copy-done
  17.3 2.9 %shard_map.47 = (f32[2,128,512]{2,1,0:T(8,128)S(1)}, f32[2,128,512]{2,1,0:T(8,128)S(1)}, f32[2,128,512]{2,1,0:T(8,128)S(1)}, f32[2,128,512]{2,1,0:T(8,128)S(1)},...) custom-call(s32[4]{0:T(128)S(1)} %copy-done.2, s32[1]{0:T(128)S(6)} %copy.5.refs_1_, ...), custom_call_target="tpu_custom_call" | custom-call | bytes 3600000 | tf_op jit(solution)/shard_map/pallas_call | solution.py:473
  20.3 0.4 collective-permute-start.1
  20.7 0.2 collective-permute-start.8
  20.9 2.6 %collective-permute-start.3 = (f32[2,256]{1,0:T(2,128)S(1)}, f32[2,256]{1,0:T(2,128)S(1)}, u32[]{:S(2)}, u32[]{:S(2)}) collective-permute-start(f32[2,256]{1,0:T(2,128)S(1)} %add.30.refs_4_), channel_id=1, source_target_pairs={{0,1},{1,0},{2,3},{3,2},{4,5},{5,4},{6,7},{7,6},{8,9},{9,8},{10,11... | collective-permute-start | bytes 6152 | tf_op jit(solution)/shard_map/ppermute | solution.py:552
  23.5 1.5 %collective-permute-done.3 = f32[2,256]{1,0:T(2,128)S(1)} collective-permute-done((f32[2,256]{1,0:T(2,128)S(1)}, f32[2,256]{1,0:T(2,128)S(1)}, u32[]{:S(2)}, u32[]{:S(2)}) %collective-permute-start.3) | collective-permute-done | bytes 2080 | tf_op jit(solution)/shard_map/ppermute | solution.py:552
  25.0 0.1 collective-permute-start.4
  25.1 2.5 %collective-permute-done.2.refs_0_.refs_3_ = f32[2,256,512]{2,1,0:T(8,128)S(1)} collective-permute-done((f32[2,256,512]{2,1,0:T(8,128)}, f32[2,256,512]{2,1,0:T(8,128)S(1)}, u32[]{:S(2)}, u32[]{:S(2)}) %collective-permute-start.2) | collective-permute-done | bytes 1048608 | tf_op jit(solution)/shard_map/ppermute | solution.py:515
  27.6 0.0 collective-permute-done.4
  27.6 0.0 collective-permute-done.1.refs_2_
  27.6 0.2 shard_map.49
  27.9 0.1 collective-permute-start.5
  28.0 0.0 collective-permute-done.8.refs_2_
  28.0 0.2 shard_map.54
  28.2 1.8 %collective-permute-start.9 = (f32[2,136,512]{2,1,0:T(8,128)S(1)}, f32[2,136,512]{2,1,0:T(8,128)S(1)}, u32[]{:S(2)}, u32[]{:S(2)}) collective-permute-start(f32[2,136,512]{2,1,0:T(8,128)S(1)} %get-tuple-element.58.refs_2_), channel_id=1, source_target_pairs={{0,254},{2,4},{4,2},{6,8},{8,6},{10,12},{12,10},{14,16},{16,14},{1... | collective-permute-start | bytes 1671176 | tf_op jit(solution)/shard_map/ppermute | solution.py:515
  30.0 0.0 collective-permute-start.6
  30.0 2.5 %collective-permute-done.6 = f32[4,256]{1,0:T(4,128)S(1)} collective-permute-done((f32[4,256]{1,0:T(4,128)S(1)}, f32[4,256]{1,0:T(4,128)S(1)}, u32[]{:S(2)}, u32[]{:S(2)}) %collective-permute-start.6) | collective-permute-done | bytes 4128 | tf_op jit(solution)/shard_map/ppermute | solution.py:515
  32.5 0.9 %collective-permute-start.10 = (f32[4,256]{1,0:T(4,128)S(1)}, f32[4,256]{1,0:T(4,128)S(1)}, u32[]{:S(2)}, u32[]{:S(2)}) collective-permute-start(f32[4,256]{1,0:T(4,128)S(1)} %add.34.refs_3_), channel_id=1, source_target_pairs={{0,128},{2,130},{4,132},{6,134},{8,136},{10,138},{12,140},{14,142}... | collective-permute-start | bytes 12296 | tf_op jit(solution)/shard_map/ppermute | solution.py:515
  33.3 3.5 %shard_map.52 = (bf16[2,768,768]{2,1,0:T(8,128)(2,1)S(1)}, bf16[2,512,1152]{2,1,0:T(8,128)(2,1)S(1)}, bf16[3,128,960]{2,1,0:T(8,128)(2,1)S(1)}, bf16[3,128,1152]...) custom-call(f32[4,256]{1,0:T(4,128)S(1)} %add_add_fusion.2.refs_4_.r, ...), custom_call_target="tpu_custom_call" | custom-call | bytes 10800000 | tf_op jit(solution)/shard_map/pallas_call | solution.py:473
  36.9 0.0 collective-permute-done.5.refs_1_
  36.9 0.2 shard_map.50
  37.2 7.3 %collective-permute-start.7 = (f32[2,8,512]{2,1,0:T(8,128)S(1)}, f32[2,8,512]{2,1,0:T(8,128)S(1)}, u32[]{:S(2)}, u32[]{:S(2)}) collective-permute-start(f32[2,8,512]{2,1,0:T(8,128)S(1)} %get-tuple-element.48), channel_id=1, source_target_pairs={{0,2},{2,0},{4,6},{6,4},{8,10},{10,8},{12,14},{14,12},{16,18},{18,... | collective-permute-start | bytes 98312 | tf_op jit(solution)/shard_map/ppermute | solution.py:515
  44.4 0.0 collective-permute-done.10
  44.4 0.0 collective-permute-start.13
  44.4 0.0 collective-permute-done.9.refs_1_
  44.4 0.2 shard_map.55
  44.7 5.3 %collective-permute-start.11 = (f32[2,8,512]{2,1,0:T(8,128)S(1)}, f32[2,8,512]{2,1,0:T(8,128)S(1)}, u32[]{:S(2)}, u32[]{:S(2)}) collective-permute-start(f32[2,8,512]{2,1,0:T(8,128)S(1)} %get-tuple-element.62), channel_id=1, source_target_pairs={{0,2},{2,0},{4,6},{6,4},{8,10},{10,8},{12,14},{14,12},{16,18},{18,... | collective-permute-start | bytes 98312 | tf_op jit(solution)/shard_map/ppermute | solution.py:515
  50.0 0.0 collective-permute-done.7.refs_2_
  50.0 0.2 shard_map.51
  50.2 2.6 %collective-permute-start.12 = (f32[2,32,768]{2,1,0:T(8,128)S(1)}, f32[2,32,768]{2,1,0:T(8,128)S(1)}, u32[]{:S(2)}, u32[]{:S(2)}) collective-permute-start(f32[2,32,768]{2,1,0:T(8,128)S(1)} %get-tuple-element.63), channel_id=1, source_target_pairs={{0,1},{1,0},{2,3},{3,2},{4,5},{5,4},{6,7},{7,6},{8,9},{9,8},{10,11... | collective-permute-start | bytes 589832 | tf_op jit(solution)/shard_map/ppermute | solution.py:594
  52.8 2.3 %shard_map.53 = (f32[3,4,128,512]{3,2,1,0:T(8,128)S(1)}, f32[3,3,128,512]{3,2,1,0:T(8,128)S(1)}, f32[4,256]{1,0:T(4,128)S(1)}) custom-call(f32[2,128,512]{2,1,0:T(8,128)S(1)} %get-tuple-element.46.refs_0_, f32[2,128,256]{2,1,0:T(8,128)S(1)} %get-tuple-element.49.refs_1_, bf16[2,768,768]{2,1,0:T(8,128)(2,1)S(1)} %get-tuple-element.50.refs_2_.refs_4_, ...), custom_call_target="tpu_custom_call" | custom-call | bytes 14400000 | tf_op jit(solution)/shard_map/pallas_call | solution.py:473
  55.0 0.0 collective-permute-done.13
  55.1 0.1 collective-permute-start.14
  55.2 3.6 %collective-permute-done.14 = f32[4,256]{1,0:T(4,128)S(1)} collective-permute-done((f32[4,256]{1,0:T(4,128)S(1)}, f32[4,256]{1,0:T(4,128)S(1)}, u32[]{:S(2)}, u32[]{:S(2)}) %collective-permute-start.14) | collective-permute-done | bytes 4128 | tf_op jit(solution)/shard_map/ppermute | solution.py:515
  58.7 0.0 collective-permute-start.15
  58.7 0.0 collective-permute-done.11.refs_2_
  58.7 0.0 collective-permute-done.12.refs_3_
  58.7 2.8 %shard_map.56 = (f32[3,4,160,512]{3,2,1,0:T(8,128)S(1)}, f32[3,3,160,512]{3,2,1,0:T(8,128)S(1)}) custom-call(f32[2,128,512]{2,1,0:T(8,128)S(1)} %get-tuple-element.60.refs_0_, f32[2,128,128]{2,1,0:T(8,128)S(1)} %get-tuple-element.61.refs_1_, f32[2,8,512]{2,1,0:T(8,128)S(1)} %collective-permute-done.11.refs_2_, ...), custom_call_target="tpu_custom_call" | custom-call | bytes 18000000 | tf_op jit(solution)/shard_map/pallas_call | solution.py:473
  61.5 3.6 %collective-permute-done.15.refs_5_ = f32[4,256]{1,0:T(4,128)S(1)} collective-permute-done((f32[4,256]{1,0:T(4,128)S(1)}, f32[4,256]{1,0:T(4,128)S(1)}, u32[]{:S(2)}, u32[]{:S(2)}) %collective-permute-start.15) | collective-permute-done | bytes 4128 | tf_op jit(solution)/shard_map/ppermute | solution.py:515
  65.1 5.6 %shard_map.57 = f32[3,256,512]{2,1,0:T(8,128)} custom-call(f32[3,4,128,512]{3,2,1,0:T(8,128)S(1)} %get-tuple-element.52.refs_0_, f32[3,3,128,512]{3,2,1,0:T(8,128)S(1)} %get-tuple-element.53.refs_1_, f32[3,4,160,512]{3,2,1,0:T(8,128)S(1)} %get-tuple-element.64.refs_2_, f32[3,3,160,512]{3,2,1,0:T(8,128)S(1)} %get-tuple-element.65.refs_3_, ...), custom_call_target="tpu_custom_call" | custom-call | bytes 36000 | tf_op jit(solution)/shard_map/pallas_call | solution.py:473
  (7 shorter events, 0.0 us)
Async XLA Ops:
  0.0 17.3 %copy-start.2 = (s32[4]{0:T(128)S(1)}, s32[4]{0:T(128)}, u32[]{:S(2)}) copy-start(s32[4]{0:T(128)} %refs_0_.3) | copy-start | bytes 52
  0.0 17.3 %copy-start.1 = (f32[4,256,512]{2,1,0:T(8,128)S(1)}, f32[4,256,512]{2,1,0:T(8,128)}, u32[]{:S(2)}) copy-start(f32[4,256,512]{2,1,0:T(8,128)} %refs_3_.3) | copy-start | bytes 6291460
  0.0 17.3 %copy-start = (s32[4,256,512]{2,1,0:T(8,128)S(1)}, s32[4,256,512]{2,1,0:T(8,128)}, u32[]{:S(2)}) copy-start(s32[4,256,512]{2,1,0:T(8,128)} %refs_2_.3) | copy-start | bytes 6291460
  5.6 22.0 %collective-permute-start.2 = (f32[2,256,512]{2,1,0:T(8,128)}, f32[2,256,512]{2,1,0:T(8,128)S(1)}, u32[]{:S(2)}, u32[]{:S(2)}) collective-permute-start(f32[2,256,512]{2,1,0:T(8,128)} %get-tuple-element.42), channel_id=1, source_target_pairs={{0,252},{2,6},{4,0},{6,10},{8,4},{10,14},{12,8},{14,18},{16,12},{1... | collective-permute-start | bytes 3145736 | tf_op jit(solution)/shard_map/ppermute | solution.py:515
  7.1 9.5 %collective-permute-start = (f32[2,256]{1,0:T(2,128)}, f32[2,256]{1,0:T(2,128)S(1)}, u32[]{:S(2)}, u32[]{:S(2)}) collective-permute-start(f32[2,256]{1,0:T(2,128)} %get-tuple-element.38), channel_id=1, source_target_pairs={{0,2},{2,0},{4,6},{6,4},{8,10},{10,8},{12,14},{14,12},{16,18},{18,... | collective-permute-start | bytes 6152 | tf_op jit(solution)/shard_map/ppermute | solution.py:515
  20.3 7.4 %collective-permute-start.1 = (f32[2,2,128,512]{3,2,1,0:T(8,128)S(1)}, f32[2,2,128,512]{3,2,1,0:T(8,128)S(1)}, u32[]{:S(2)}, u32[]{:S(2)}) collective-permute-start(f32[2,2,128,512]{3,2,1,0:T(8,128)S(1)} %get-tuple-element.41), channel_id=1, source_target_pairs={{0,2},{2,0},{4,6},{6,4},{8,10},{10,8},{12,14},{14,12},{16,18},{18,... | collective-permute-start | bytes 3145736 | tf_op jit(solution)/shard_map/ppermute | solution.py:515
  20.7 7.3 %collective-permute-start.8 = (f32[2,2,128,512]{3,2,1,0:T(8,128)S(1)}, f32[2,2,128,512]{3,2,1,0:T(8,128)S(1)}, u32[]{:S(2)}, u32[]{:S(2)}) collective-permute-start(f32[2,2,128,512]{3,2,1,0:T(8,128)S(1)} %get-tuple-element.56), channel_id=1, source_target_pairs={{0,2},{2,0},{4,6},{6,4},{8,10},{10,8},{12,14},{14,12},{16,18},{18,... | collective-permute-start | bytes 3145736 | tf_op jit(solution)/shard_map/ppermute | solution.py:515
  20.9 4.1 %collective-permute-start.3 = (f32[2,256]{1,0:T(2,128)S(1)}, f32[2,256]{1,0:T(2,128)S(1)}, u32[]{:S(2)}, u32[]{:S(2)}) collective-permute-start(f32[2,256]{1,0:T(2,128)S(1)} %add.30.refs_4_), channel_id=1, source_target_pairs={{0,1},{1,0},{2,3},{3,2},{4,5},{5,4},{6,7},{7,6},{8,9},{9,8},{10,11... | collective-permute-start | bytes 6152 | tf_op jit(solution)/shard_map/ppermute | solution.py:552
  25.0 2.6 %collective-permute-start.4 = (f32[4,256]{1,0:T(4,128)S(1)}, f32[4,256]{1,0:T(4,128)S(1)}, u32[]{:S(2)}, u32[]{:S(2)}) collective-permute-start(f32[4,256]{1,0:T(4,128)S(1)} %maximum_add_fusion), channel_id=1, source_target_pairs={{0,32},{2,34},{4,36},{6,38},{8,40},{10,42},{12,44},{14,46},{16,48}... | collective-permute-start | bytes 12296 | tf_op jit(solution)/shard_map/ppermute | solution.py:515
  27.9 9.0 %collective-permute-start.5 = (f32[2,136,512]{2,1,0:T(8,128)S(1)}, f32[2,136,512]{2,1,0:T(8,128)S(1)}, u32[]{:S(2)}, u32[]{:S(2)}) collective-permute-start(f32[2,136,512]{2,1,0:T(8,128)S(1)} %get-tuple-element.45.refs_2_), channel_id=1, source_target_pairs={{0,254},{2,4},{4,2},{6,8},{8,6},{10,12},{12,10},{14,16},{16,14},{1... | collective-permute-start | bytes 1671176 | tf_op jit(solution)/shard_map/ppermute | solution.py:515
  28.2 16.3 %collective-permute-start.9 = (f32[2,136,512]{2,1,0:T(8,128)S(1)}, f32[2,136,512]{2,1,0:T(8,128)S(1)}, u32[]{:S(2)}, u32[]{:S(2)}) collective-permute-start(f32[2,136,512]{2,1,0:T(8,128)S(1)} %get-tuple-element.58.refs_2_), channel_id=1, source_target_pairs={{0,254},{2,4},{4,2},{6,8},{8,6},{10,12},{12,10},{14,16},{16,14},{1... | collective-permute-start | bytes 1671176 | tf_op jit(solution)/shard_map/ppermute | solution.py:515
  30.0 2.5 %collective-permute-start.6 = (f32[4,256]{1,0:T(4,128)S(1)}, f32[4,256]{1,0:T(4,128)S(1)}, u32[]{:S(2)}, u32[]{:S(2)}) collective-permute-start(f32[4,256]{1,0:T(4,128)S(1)} %add_add_fusion.2.refs_4_.refs_0_), channel_id=1, source_target_pairs={{0,64},{2,66},{4,68},{6,70},{8,72},{10,74},{12,76},{14,78},{16,80}... | collective-permute-start | bytes 12296 | tf_op jit(solution)/shard_map/ppermute | solution.py:515
  32.5 12.0 %collective-permute-start.10 = (f32[4,256]{1,0:T(4,128)S(1)}, f32[4,256]{1,0:T(4,128)S(1)}, u32[]{:S(2)}, u32[]{:S(2)}) collective-permute-start(f32[4,256]{1,0:T(4,128)S(1)} %add.34.refs_3_), channel_id=1, source_target_pairs={{0,128},{2,130},{4,132},{6,134},{8,136},{10,138},{12,140},{14,142}... | collective-permute-start | bytes 12296 | tf_op jit(solution)/shard_map/ppermute | solution.py:515
  37.2 12.8 %collective-permute-start.7 = (f32[2,8,512]{2,1,0:T(8,128)S(1)}, f32[2,8,512]{2,1,0:T(8,128)S(1)}, u32[]{:S(2)}, u32[]{:S(2)}) collective-permute-start(f32[2,8,512]{2,1,0:T(8,128)S(1)} %get-tuple-element.48), channel_id=1, source_target_pairs={{0,2},{2,0},{4,6},{6,4},{8,10},{10,8},{12,14},{14,12},{16,18},{18,... | collective-permute-start | bytes 98312 | tf_op jit(solution)/shard_map/ppermute | solution.py:515
  44.4 10.6 %collective-permute-start.13 = (f32[4,256]{1,0:T(4,128)S(1)}, f32[4,256]{1,0:T(4,128)S(1)}, u32[]{:S(2)}, u32[]{:S(2)}) collective-permute-start(f32[4,256]{1,0:T(4,128)S(1)} %add_add_fusion.1.refs_3_), channel_id=1, source_target_pairs={{0,4},{2,6},{4,0},{6,2},{8,12},{10,14},{12,8},{14,10},{16,20},{18,... | collective-permute-start | bytes 12296 | tf_op jit(solution)/shard_map/ppermute | solution.py:515
  44.7 14.0 %collective-permute-start.11 = (f32[2,8,512]{2,1,0:T(8,128)S(1)}, f32[2,8,512]{2,1,0:T(8,128)S(1)}, u32[]{:S(2)}, u32[]{:S(2)}) collective-permute-start(f32[2,8,512]{2,1,0:T(8,128)S(1)} %get-tuple-element.62), channel_id=1, source_target_pairs={{0,2},{2,0},{4,6},{6,4},{8,10},{10,8},{12,14},{14,12},{16,18},{18,... | collective-permute-start | bytes 98312 | tf_op jit(solution)/shard_map/ppermute | solution.py:515
  50.2 8.5 %collective-permute-start.12 = (f32[2,32,768]{2,1,0:T(8,128)S(1)}, f32[2,32,768]{2,1,0:T(8,128)S(1)}, u32[]{:S(2)}, u32[]{:S(2)}) collective-permute-start(f32[2,32,768]{2,1,0:T(8,128)S(1)} %get-tuple-element.63), channel_id=1, source_target_pairs={{0,1},{1,0},{2,3},{3,2},{4,5},{5,4},{6,7},{7,6},{8,9},{9,8},{10,11... | collective-permute-start | bytes 589832 | tf_op jit(solution)/shard_map/ppermute | solution.py:594
  55.1 3.7 %collective-permute-start.14 = (f32[4,256]{1,0:T(4,128)S(1)}, f32[4,256]{1,0:T(4,128)S(1)}, u32[]{:S(2)}, u32[]{:S(2)}) collective-permute-start(f32[4,256]{1,0:T(4,128)S(1)} %add_add_fusion), channel_id=1, source_target_pairs={{0,8},{2,10},{4,12},{6,14},{8,0},{10,2},{12,4},{14,6},{16,24},{18,... | collective-permute-start | bytes 12296 | tf_op jit(solution)/shard_map/ppermute | solution.py:515
  58.7 6.4 %collective-permute-start.15 = (f32[4,256]{1,0:T(4,128)S(1)}, f32[4,256]{1,0:T(4,128)S(1)}, u32[]{:S(2)}, u32[]{:S(2)}) collective-permute-start(f32[4,256]{1,0:T(4,128)S(1)} %add.39.refs_4_), channel_id=1, source_target_pairs={{0,16},{2,18},{4,20},{6,22},{8,24},{10,26},{12,28},{14,30},{16,0},... | collective-permute-start | bytes 12296 | tf_op jit(solution)/shard_map/ppermute | solution.py:515
